TPU v7x, 128 devices: a whole 4x4x4 slice. The times are simulated.
128 devices in a mesh: seq: 32 (over y, x, core), tp: 4 (over z).
Axes of the slice: x: 4, y: 4, z: 4, core: 2. Of those that a mesh axis runs over, the one named last changes fastest.
Arguments:
- projected: bfloat16 [18560, 32768], P(('tp', 'seq')), may hold values from -4 to 98
- conv_weight: float32 [4, 8, 1280], P(None, 'tp'), may hold values from -3 to 3
- dt_bias: float32 [128], P('tp'), may hold values from -7 to -1
- a_log: float32 [128], P('tp'), may hold values from -7 to -1
- d_skip: float32 [128], P('tp'), may hold values from 0.5 to 2
- norm_gain: float32 [8192], P('tp'), may hold values from 0.25 to 1.75
Outputs:
- mixer_out: bfloat16 [32768, 8192], P('seq', 'tp')
All inputs are finite; a program needn't handle non-finite values.
Results may differ from a plain program's by a relative error of at most 0.0034.
Values may be sent and summed in bfloat16 or wider, within the bound.
A program may use at most 192 MiB of HBM per device.

v0:
```python
import jax
import jax.numpy as jnp
from jax import lax
from jax.sharding import PartitionSpec as P

HEAD_DIM = 64
STATE_WIDTH = 128
BLOCK = 256


epsilon = 1e-05


def passed_along(shard, axis, by):
    count = lax.axis_size(axis)
    pairs = [(i, i + by) for i in range(count) if 0 <= i + by < count]
    return lax.ppermute(shard, axis, pairs)


def block_step(state_now, pieces):
    block_values, block_input, block_output, block_decay, block_steps = pieces
    running = jnp.cumsum(block_decay, axis=0)
    length = running.shape[0]
    scores = jnp.einsum(
        "tgn,sgn->gts", block_output, block_input, preferred_element_type=jnp.float32
    )
    running_heads = jnp.transpose(running, (1, 2, 0))
    log_gaps = running_heads[:, :, :, None] - running_heads[:, :, None, :]
    row_index = lax.broadcasted_iota(jnp.int32, (length, length), 0)
    col_index = lax.broadcasted_iota(jnp.int32, (length, length), 1)
    decays = jnp.exp(jnp.where(row_index >= col_index, log_gaps, -jnp.inf))
    weights = (
        scores[:, None] * decays * jnp.transpose(block_steps, (1, 2, 0))[:, :, None, :]
    ).astype(jnp.bfloat16)
    intra_part = jnp.einsum(
        "gjts,sgjp->tgjp", weights, block_values, preferred_element_type=jnp.float32
    )
    block_end = running[-1]
    carry_scale = jnp.exp(block_end[None] - running) * block_steps
    weighted = (block_values * carry_scale[..., None]).astype(jnp.bfloat16)
    update = jnp.einsum("sgjp,sgn->gjpn", weighted, block_input, preferred_element_type=jnp.float32)
    advanced = jnp.exp(block_end)[..., None, None] * state_now + update
    return (advanced, (state_now, intra_part, running))


def per_device(projected, conv_weight, dt_bias, a_log, d_skip, norm_gain):
    seq_count = lax.axis_size("seq")
    tap_count = conv_weight.shape[0]
    group_count = conv_weight.shape[1]
    conv_channels = conv_weight.shape[2]
    head_count = dt_bias.shape[0]
    heads_group = head_count // group_count
    group_span_width = heads_group * HEAD_DIM
    group_cols = 2 * group_span_width + 2 * STATE_WIDTH + heads_group
    slice_width, all_tokens = projected.shape
    local_tokens = all_tokens // seq_count
    received_rows = lax.all_to_all(projected, "seq", split_axis=1, concat_axis=0, tiled=True)
    columns = jnp.transpose(received_rows).reshape(local_tokens, group_count, group_cols)
    conv_input = columns[:, :, group_span_width : group_span_width + conv_channels]
    rim_rows = passed_along(conv_input[local_tokens - (tap_count - 1) :], "seq", 1)
    padded = jnp.concatenate([rim_rows, conv_input], axis=0)
    summed = conv_weight[0] * padded[0:local_tokens]
    for tap_index in range(1, tap_count):
        summed = summed + conv_weight[tap_index] * padded[tap_index : tap_index + local_tokens]
    activated = jax.nn.silu(summed).astype(jnp.bfloat16)
    gate_part = columns[:, :, :group_span_width]
    step_raw = columns[:, :, group_span_width + conv_channels :].astype(jnp.float32)
    head_values = activated[:, :, :group_span_width].reshape(
        local_tokens, group_count, heads_group, HEAD_DIM
    )
    input_map = activated[:, :, group_span_width : group_span_width + STATE_WIDTH]
    output_map = activated[:, :, group_span_width + STATE_WIDTH :]
    step_size = jax.nn.softplus(step_raw + dt_bias.reshape(group_count, heads_group))
    log_decay = -jnp.exp(a_log).reshape(group_count, heads_group) * step_size
    block_count = local_tokens // BLOCK

    def to_blocks(tensor):
        return tensor.reshape((block_count, BLOCK) + tensor.shape[1:])

    zero_state = jnp.zeros((group_count, heads_group, HEAD_DIM, STATE_WIDTH), jnp.float32)
    device_state, (block_states, intra_parts, running) = lax.scan(
        block_step,
        zero_state,
        (
            to_blocks(head_values),
            to_blocks(input_map),
            to_blocks(output_map),
            to_blocks(log_decay),
            to_blocks(step_size),
        ),
    )
    block_ends = running[:, -1]
    device_decay = jnp.exp(jnp.sum(block_ends, axis=0))
    lead_in = jnp.cumsum(block_ends, axis=0) - block_ends

    def relay_step(turn_index, carried):
        received = passed_along(carried[1], "seq", 1)
        return (received, device_decay[..., None, None] * received + device_state)

    incoming = lax.fori_loop(0, seq_count - 1, relay_step, (zero_state, device_state))[0]
    full_states = block_states + jnp.exp(lead_in)[..., None, None] * incoming[None]
    carried_part = jnp.exp(running)[..., None] * jnp.einsum(
        "ktgn,kgjpn->ktgjp",
        to_blocks(output_map).astype(jnp.float32),
        full_states,
        precision=lax.Precision.HIGHEST,
    )
    mixed_out = (intra_parts + carried_part).reshape(
        local_tokens, group_count, heads_group, HEAD_DIM
    ) + d_skip.reshape(group_count, heads_group)[:, :, None] * head_values.astype(jnp.float32)
    gated_out = mixed_out.reshape(local_tokens, group_count, group_span_width) * jax.nn.silu(
        gate_part.astype(jnp.float32)
    )
    mean_square = jnp.mean(gated_out * gated_out, axis=-1, keepdims=True)
    normed = (
        gated_out
        * lax.rsqrt(mean_square + epsilon)
        * norm_gain.reshape(group_count, group_span_width)
    )
    return normed.reshape(local_tokens, group_count * group_span_width).astype(jnp.bfloat16)


def solution(mesh):
    in_specs = (P(("tp", "seq"), None), P(None, "tp", None), P("tp"), P("tp"), P("tp"), P("tp"))
    out_specs = P("seq", "tp")
    return jax.shard_map(
        per_device, mesh=mesh, in_specs=in_specs, out_specs=out_specs, check_vma=False
    )
```

profile of v0, /device:TPU:112, one launch (start us, length us, event | category | flops | bytes accessed | tf_op | source)
XLA Modules:
  0.0 929.9 jit_solution(3226702151961235112)
XLA Ops:
  0.0 14.4 %copy.72 = bf16[19,8,32,1024]{3,2,1,0:T(8,128)(2,1)} copy(bf16[19,8,32,1024]{3,1,2,0:T(8,128)(2,1)} %bitcast.149) | data formatting | bytes 19922944
  14.4 9.5 %slice.87 = bf16[145,32,1024]{2,1,0:T(8,128)(2,1)} slice(bf16[152,32,1024]{2,1,0:T(8,128)(2,1)} %bitcast.147), slice={[0:145], [0:32], [0:1024]} | slice | bytes 19005440 | tf_op jit(solution)/shard_map/all_to_all | solution.py:57
  23.9 13.1 %copy.49 = bf16[145,32,1024]{2,0,1:T(8,128)(2,1)} copy(bf16[145,32,1024]{2,1,0:T(8,128)(2,1)} %slice.87) | data formatting | bytes 19005440 | tf_op jit(solution)/shard_map/all_to_all | solution.py:57
  37.0 7.6 all-to-all-start
  45.1 123.2 %all-to-all-done = bf16[145,32,1024]{2,0,1:T(8,128)(2,1)} async-done(((bf16[145,32,1024]{2,0,1:T(8,128)(2,1)}), bf16[145,32,1024]{2,0,1:T(8,128)(2,1)}, u32[]{:S(2)}, u32[]{:S(2)}) %all-to-all-start) | async-done | bytes 9502752 | tf_op jit(solution)/shard_map/all_to_all | solution.py:57
  168.3 8.7 all_to_all.17
  178.7 1.9 collective-permute-start.1
  181.6 5.4 slice.78
  187.5 16.5 %multiply_convert_fusion.6 = bf16[1024,2,1280]{0,2,1:T(8,128)(2,1)S(1)} fusion(bf16[1024,2,1280]{0,2,1:T(8,128)(2,1)} %slice.78, bf16[3,2,1280]{0,2,1:T(8,128)(2,1)S(1)} %copy.51, f32[2,1280]{1,0:T(2,128)S(1)} %get-tuple-element.208, f32[2,1280]{1,0:T(2,128)S(1)} %get-tuple-element.209, f32[2,1280]{1,0:T(2,128)S(1)} %get-tuple-element.207, ...), kind=kLoop, calls=%fused_computation.44 | loop fusion | flops 65536000 | bytes 10542080 | tf_op jit(solution)/shard_map/convert_element_type | solution.py:65
  204.2 2.2 copy-done
  206.4 2.4 slice.83
  209.3 7.9 reshape_reshape.3
  217.1 4.9 copy.55
  222.1 38.9 %while.30 = (s32[]{:T(128)}, f32[2,16,64,128]{3,2,1,0:T(8,128)S(1)}, f32[4,2,16,64,128]{4,3,2,1,0:T(8,128)}, f32[4,256,2,16,64]{1,4,3,2,0:T(8,128)}, f32[4,256,2...) while((s32[]{:T(128)}, ...), condition=%wide.region_3.4_spmd.clone, body=%wide.region_0.3_spmd.clone.sunk | while | flops 450461792 | bytes 10693016 | solution.py:81
  223.9 4.5 bitcast_dynamic-update-slice_fusion.5
  233.6 4.5 bitcast_dynamic-update-slice_fusion.5
  243.3 4.6 bitcast_dynamic-update-slice_fusion.5
  253.1 4.5 bitcast_dynamic-update-slice_fusion.5
  262.2 613.8 %while.29 = (s32[]{:T(128)}, f32[2,16,64,128]{3,2,1,0:T(8,128)}, f32[2,16,64,128]{3,2,1,0:T(8,128)}, f32[2,16]{1,0:T(2,128)S(1)}, f32[2,16,64,128]{3,2,1,0:T(8,128)S(1)}, /*index=5*/s32[]{:T(128)}) while((s32[]{:T(128)}, f32[2,16,64,128]{3,2,1,0:T(8,128)}, f32[2,16,64,128]{3,2,1,0:T(8,128)}, f32[2,16]{1,0:T(2,128)S(1)}, ...), condition=%wide.region_7.8_spmd, body=%wide.region_6.7_spmd.sunk | while | flops 524290 | bytes 11534601 | solution.py:100
  262.2 1.9 collective-permute-start
  264.1 16.5 %collective-permute-done = f32[2,16,64,128]{3,2,1,0:T(8,128)S(1)} collective-permute-done((f32[2,16,64,128]{3,2,1,0:T(8,128)}, f32[2,16,64,128]{3,2,1,0:T(8,128)S(1)}, u32[]{:S(2)}, u32[]{:S(2)}) %collective-permute-start) | collective-permute-done | bytes 1048608 | tf_op jit(solution)/shard_map/while/body/eval_jaxpr/ppermute | solution.py:17
  282.0 1.9 collective-permute-start
  283.9 16.5 %collective-permute-done = f32[2,16,64,128]{3,2,1,0:T(8,128)S(1)} collective-permute-done((f32[2,16,64,128]{3,2,1,0:T(8,128)}, f32[2,16,64,128]{3,2,1,0:T(8,128)S(1)}, u32[]{:S(2)}, u32[]{:S(2)}) %collective-permute-start) | collective-permute-done | bytes 1048608 | tf_op jit(solution)/shard_map/while/body/eval_jaxpr/ppermute | solution.py:17
  303.7 16.5 %collective-permute-done = f32[2,16,64,128]{3,2,1,0:T(8,128)S(1)} collective-permute-done((f32[2,16,64,128]{3,2,1,0:T(8,128)}, f32[2,16,64,128]{3,2,1,0:T(8,128)S(1)}, u32[]{:S(2)}, u32[]{:S(2)}) %collective-permute-start) | collective-permute-done | bytes 1048608 | tf_op jit(solution)/shard_map/while/body/eval_jaxpr/ppermute | solution.py:17
  321.6 1.9 collective-permute-start
  323.5 16.5 %collective-permute-done = f32[2,16,64,128]{3,2,1,0:T(8,128)S(1)} collective-permute-done((f32[2,16,64,128]{3,2,1,0:T(8,128)}, f32[2,16,64,128]{3,2,1,0:T(8,128)S(1)}, u32[]{:S(2)}, u32[]{:S(2)}) %collective-permute-start) | collective-permute-done | bytes 1048608 | tf_op jit(solution)/shard_map/while/body/eval_jaxpr/ppermute | solution.py:17
  343.3 16.5 %collective-permute-done = f32[2,16,64,128]{3,2,1,0:T(8,128)S(1)} collective-permute-done((f32[2,16,64,128]{3,2,1,0:T(8,128)}, f32[2,16,64,128]{3,2,1,0:T(8,128)S(1)}, u32[]{:S(2)}, u32[]{:S(2)}) %collective-permute-start) | collective-permute-done | bytes 1048608 | tf_op jit(solution)/shard_map/while/body/eval_jaxpr/ppermute | solution.py:17
  361.2 1.9 collective-permute-start
  363.1 16.5 %collective-permute-done = f32[2,16,64,128]{3,2,1,0:T(8,128)S(1)} collective-permute-done((f32[2,16,64,128]{3,2,1,0:T(8,128)}, f32[2,16,64,128]{3,2,1,0:T(8,128)S(1)}, u32[]{:S(2)}, u32[]{:S(2)}) %collective-permute-start) | collective-permute-done | bytes 1048608 | tf_op jit(solution)/shard_map/while/body/eval_jaxpr/ppermute | solution.py:17
  382.9 16.5 %collective-permute-done = f32[2,16,64,128]{3,2,1,0:T(8,128)S(1)} collective-permute-done((f32[2,16,64,128]{3,2,1,0:T(8,128)}, f32[2,16,64,128]{3,2,1,0:T(8,128)S(1)}, u32[]{:S(2)}, u32[]{:S(2)}) %collective-permute-start) | collective-permute-done | bytes 1048608 | tf_op jit(solution)/shard_map/while/body/eval_jaxpr/ppermute | solution.py:17
  400.8 1.9 collective-permute-start
  402.7 16.5 %collective-permute-done = f32[2,16,64,128]{3,2,1,0:T(8,128)S(1)} collective-permute-done((f32[2,16,64,128]{3,2,1,0:T(8,128)}, f32[2,16,64,128]{3,2,1,0:T(8,128)S(1)}, u32[]{:S(2)}, u32[]{:S(2)}) %collective-permute-start) | collective-permute-done | bytes 1048608 | tf_op jit(solution)/shard_map/while/body/eval_jaxpr/ppermute | solution.py:17
  420.5 1.9 collective-permute-start
  422.5 16.5 %collective-permute-done = f32[2,16,64,128]{3,2,1,0:T(8,128)S(1)} collective-permute-done((f32[2,16,64,128]{3,2,1,0:T(8,128)}, f32[2,16,64,128]{3,2,1,0:T(8,128)S(1)}, u32[]{:S(2)}, u32[]{:S(2)}) %collective-permute-start) | collective-permute-done | bytes 1048608 | tf_op jit(solution)/shard_map/while/body/eval_jaxpr/ppermute | solution.py:17
  440.3 1.9 collective-permute-start
  442.3 16.5 %collective-permute-done = f32[2,16,64,128]{3,2,1,0:T(8,128)S(1)} collective-permute-done((f32[2,16,64,128]{3,2,1,0:T(8,128)}, f32[2,16,64,128]{3,2,1,0:T(8,128)S(1)}, u32[]{:S(2)}, u32[]{:S(2)}) %collective-permute-start) | collective-permute-done | bytes 1048608 | tf_op jit(solution)/shard_map/while/body/eval_jaxpr/ppermute | solution.py:17
  460.1 1.9 collective-permute-start
  462.0 16.5 %collective-permute-done = f32[2,16,64,128]{3,2,1,0:T(8,128)S(1)} collective-permute-done((f32[2,16,64,128]{3,2,1,0:T(8,128)}, f32[2,16,64,128]{3,2,1,0:T(8,128)S(1)}, u32[]{:S(2)}, u32[]{:S(2)}) %collective-permute-start) | collective-permute-done | bytes 1048608 | tf_op jit(solution)/shard_map/while/body/eval_jaxpr/ppermute | solution.py:17
  481.8 16.5 %collective-permute-done = f32[2,16,64,128]{3,2,1,0:T(8,128)S(1)} collective-permute-done((f32[2,16,64,128]{3,2,1,0:T(8,128)}, f32[2,16,64,128]{3,2,1,0:T(8,128)S(1)}, u32[]{:S(2)}, u32[]{:S(2)}) %collective-permute-start) | collective-permute-done | bytes 1048608 | tf_op jit(solution)/shard_map/while/body/eval_jaxpr/ppermute | solution.py:17
  501.6 16.5 %collective-permute-done = f32[2,16,64,128]{3,2,1,0:T(8,128)S(1)} collective-permute-done((f32[2,16,64,128]{3,2,1,0:T(8,128)}, f32[2,16,64,128]{3,2,1,0:T(8,128)S(1)}, u32[]{:S(2)}, u32[]{:S(2)}) %collective-permute-start) | collective-permute-done | bytes 1048608 | tf_op jit(solution)/shard_map/while/body/eval_jaxpr/ppermute | solution.py:17
  521.4 16.5 %collective-permute-done = f32[2,16,64,128]{3,2,1,0:T(8,128)S(1)} collective-permute-done((f32[2,16,64,128]{3,2,1,0:T(8,128)}, f32[2,16,64,128]{3,2,1,0:T(8,128)S(1)}, u32[]{:S(2)}, u32[]{:S(2)}) %collective-permute-start) | collective-permute-done | bytes 1048608 | tf_op jit(solution)/shard_map/while/body/eval_jaxpr/ppermute | solution.py:17
  541.2 16.5 %collective-permute-done = f32[2,16,64,128]{3,2,1,0:T(8,128)S(1)} collective-permute-done((f32[2,16,64,128]{3,2,1,0:T(8,128)}, f32[2,16,64,128]{3,2,1,0:T(8,128)S(1)}, u32[]{:S(2)}, u32[]{:S(2)}) %collective-permute-start) | collective-permute-done | bytes 1048608 | tf_op jit(solution)/shard_map/while/body/eval_jaxpr/ppermute | solution.py:17
  561.0 16.5 %collective-permute-done = f32[2,16,64,128]{3,2,1,0:T(8,128)S(1)} collective-permute-done((f32[2,16,64,128]{3,2,1,0:T(8,128)}, f32[2,16,64,128]{3,2,1,0:T(8,128)S(1)}, u32[]{:S(2)}, u32[]{:S(2)}) %collective-permute-start) | collective-permute-done | bytes 1048608 | tf_op jit(solution)/shard_map/while/body/eval_jaxpr/ppermute | solution.py:17
  580.8 16.5 %collective-permute-done = f32[2,16,64,128]{3,2,1,0:T(8,128)S(1)} collective-permute-done((f32[2,16,64,128]{3,2,1,0:T(8,128)}, f32[2,16,64,128]{3,2,1,0:T(8,128)S(1)}, u32[]{:S(2)}, u32[]{:S(2)}) %collective-permute-start) | collective-permute-done | bytes 1048608 | tf_op jit(solution)/shard_map/while/body/eval_jaxpr/ppermute | solution.py:17
  600.6 16.5 %collective-permute-done = f32[2,16,64,128]{3,2,1,0:T(8,128)S(1)} collective-permute-done((f32[2,16,64,128]{3,2,1,0:T(8,128)}, f32[2,16,64,128]{3,2,1,0:T(8,128)S(1)}, u32[]{:S(2)}, u32[]{:S(2)}) %collective-permute-start) | collective-permute-done | bytes 1048608 | tf_op jit(solution)/shard_map/while/body/eval_jaxpr/ppermute | solution.py:17
  620.4 16.5 %collective-permute-done = f32[2,16,64,128]{3,2,1,0:T(8,128)S(1)} collective-permute-done((f32[2,16,64,128]{3,2,1,0:T(8,128)}, f32[2,16,64,128]{3,2,1,0:T(8,128)S(1)}, u32[]{:S(2)}, u32[]{:S(2)}) %collective-permute-start) | collective-permute-done | bytes 1048608 | tf_op jit(solution)/shard_map/while/body/eval_jaxpr/ppermute | solution.py:17
  640.2 16.5 %collective-permute-done = f32[2,16,64,128]{3,2,1,0:T(8,128)S(1)} collective-permute-done((f32[2,16,64,128]{3,2,1,0:T(8,128)}, f32[2,16,64,128]{3,2,1,0:T(8,128)S(1)}, u32[]{:S(2)}, u32[]{:S(2)}) %collective-permute-start) | collective-permute-done | bytes 1048608 | tf_op jit(solution)/shard_map/while/body/eval_jaxpr/ppermute | solution.py:17
  660.0 16.5 %collective-permute-done = f32[2,16,64,128]{3,2,1,0:T(8,128)S(1)} collective-permute-done((f32[2,16,64,128]{3,2,1,0:T(8,128)}, f32[2,16,64,128]{3,2,1,0:T(8,128)S(1)}, u32[]{:S(2)}, u32[]{:S(2)}) %collective-permute-start) | collective-permute-done | bytes 1048608 | tf_op jit(solution)/shard_map/while/body/eval_jaxpr/ppermute | solution.py:17
  679.8 16.5 %collective-permute-done = f32[2,16,64,128]{3,2,1,0:T(8,128)S(1)} collective-permute-done((f32[2,16,64,128]{3,2,1,0:T(8,128)}, f32[2,16,64,128]{3,2,1,0:T(8,128)S(1)}, u32[]{:S(2)}, u32[]{:S(2)}) %collective-permute-start) | collective-permute-done | bytes 1048608 | tf_op jit(solution)/shard_map/while/body/eval_jaxpr/ppermute | solution.py:17
  699.6 16.5 %collective-permute-done = f32[2,16,64,128]{3,2,1,0:T(8,128)S(1)} collective-permute-done((f32[2,16,64,128]{3,2,1,0:T(8,128)}, f32[2,16,64,128]{3,2,1,0:T(8,128)S(1)}, u32[]{:S(2)}, u32[]{:S(2)}) %collective-permute-start) | collective-permute-done | bytes 1048608 | tf_op jit(solution)/shard_map/while/body/eval_jaxpr/ppermute | solution.py:17
  719.4 16.5 %collective-permute-done = f32[2,16,64,128]{3,2,1,0:T(8,128)S(1)} collective-permute-done((f32[2,16,64,128]{3,2,1,0:T(8,128)}, f32[2,16,64,128]{3,2,1,0:T(8,128)S(1)}, u32[]{:S(2)}, u32[]{:S(2)}) %collective-permute-start) | collective-permute-done | bytes 1048608 | tf_op jit(solution)/shard_map/while/body/eval_jaxpr/ppermute | solution.py:17
  739.2 16.5 %collective-permute-done = f32[2,16,64,128]{3,2,1,0:T(8,128)S(1)} collective-permute-done((f32[2,16,64,128]{3,2,1,0:T(8,128)}, f32[2,16,64,128]{3,2,1,0:T(8,128)S(1)}, u32[]{:S(2)}, u32[]{:S(2)}) %collective-permute-start) | collective-permute-done | bytes 1048608 | tf_op jit(solution)/shard_map/while/body/eval_jaxpr/ppermute | solution.py:17
  759.0 16.5 %collective-permute-done = f32[2,16,64,128]{3,2,1,0:T(8,128)S(1)} collective-permute-done((f32[2,16,64,128]{3,2,1,0:T(8,128)}, f32[2,16,64,128]{3,2,1,0:T(8,128)S(1)}, u32[]{:S(2)}, u32[]{:S(2)}) %collective-permute-start) | collective-permute-done | bytes 1048608 | tf_op jit(solution)/shard_map/while/body/eval_jaxpr/ppermute | solution.py:17
  778.8 16.5 %collective-permute-done = f32[2,16,64,128]{3,2,1,0:T(8,128)S(1)} collective-permute-done((f32[2,16,64,128]{3,2,1,0:T(8,128)}, f32[2,16,64,128]{3,2,1,0:T(8,128)S(1)}, u32[]{:S(2)}, u32[]{:S(2)}) %collective-permute-start) | collective-permute-done | bytes 1048608 | tf_op jit(solution)/shard_map/while/body/eval_jaxpr/ppermute | solution.py:17
  798.5 16.5 %collective-permute-done = f32[2,16,64,128]{3,2,1,0:T(8,128)S(1)} collective-permute-done((f32[2,16,64,128]{3,2,1,0:T(8,128)}, f32[2,16,64,128]{3,2,1,0:T(8,128)S(1)}, u32[]{:S(2)}, u32[]{:S(2)}) %collective-permute-start) | collective-permute-done | bytes 1048608 | tf_op jit(solution)/shard_map/while/body/eval_jaxpr/ppermute | solution.py:17
  818.3 16.5 %collective-permute-done = f32[2,16,64,128]{3,2,1,0:T(8,128)S(1)} collective-permute-done((f32[2,16,64,128]{3,2,1,0:T(8,128)}, f32[2,16,64,128]{3,2,1,0:T(8,128)S(1)}, u32[]{:S(2)}, u32[]{:S(2)}) %collective-permute-start) | collective-permute-done | bytes 1048608 | tf_op jit(solution)/shard_map/while/body/eval_jaxpr/ppermute | solution.py:17
  838.1 16.5 %collective-permute-done = f32[2,16,64,128]{3,2,1,0:T(8,128)S(1)} collective-permute-done((f32[2,16,64,128]{3,2,1,0:T(8,128)}, f32[2,16,64,128]{3,2,1,0:T(8,128)S(1)}, u32[]{:S(2)}, u32[]{:S(2)}) %collective-permute-start) | collective-permute-done | bytes 1048608 | tf_op jit(solution)/shard_map/while/body/eval_jaxpr/ppermute | solution.py:17
  857.9 16.5 %collective-permute-done = f32[2,16,64,128]{3,2,1,0:T(8,128)S(1)} collective-permute-done((f32[2,16,64,128]{3,2,1,0:T(8,128)}, f32[2,16,64,128]{3,2,1,0:T(8,128)S(1)}, u32[]{:S(2)}, u32[]{:S(2)}) %collective-permute-start) | collective-permute-done | bytes 1048608 | tf_op jit(solution)/shard_map/while/body/eval_jaxpr/ppermute | solution.py:17
  876.0 12.0 %fusion.28 = f32[4,256,2,16,64]{1,4,3,2,0:T(8,128)} fusion(f32[4,256,2,16,64]{1,4,3,2,0:T(8,128)} %get-tuple-element.86, f32[4,256,2,16]{1,3,2,0:T(8,128)S(1)} %exp.44, f32[4,2,16,64,128]{4,3,2,1,0:T(8,128)} %get-tuple-element.88, f32[2,16,64,128]{3,2,1,0:T(8,128)} %get-tuple-element.90, f32[4,2,16]{2,1,0:T(2,128)S(1)} %fusion.38, ...), kind=kOutput, calls=%fused_computation.50 | convolution fusion | flops 3227516928 | bytes 22675968 | tf_op jit(solution)/shard_map/ktgn,kgjpn->ktgjp/dot_general | solution.py:102
  888.0 13.9 %copy.60 = f32[4,256,2,16,64]{1,0,4,3,2:T(4,128)} copy(f32[4,256,2,16,64]{1,4,3,2,0:T(8,128)} %fusion.28) | data formatting | bytes 16777216 | tf_op jit(solution)/shard_map/add | solution.py:108
  901.9 10.7 %reshape.87 = f32[1024,2,1024]{0,2,1:T(8,128)} reshape(f32[4,256,2,16,64]{1,0,4,3,2:T(4,128)} %copy.60) | data formatting | bytes 16777216 | tf_op jit(solution)/shard_map/reshape | solution.py:108
  912.7 8.0 multiply_reduce_fusion
  920.7 2.4 multiply_convert_fusion.7
  923.0 6.4 copy.61
  (228 shorter events, 112.2 us)
Async XLA Ops:
  37.0 7.7 copy-start.4
  37.0 7.8 copy-start.5
  37.0 7.9 copy-start.6
  37.0 8.1 copy-start.3
  37.0 8.1 copy-start.2
  37.0 131.3 %all-to-all-start = ((bf16[145,32,1024]{2,0,1:T(8,128)(2,1)}), bf16[145,32,1024]{2,0,1:T(8,128)(2,1)}, u32[]{:S(2)}, u32[]{:S(2)}) async-start(bf16[145,32,1024]{2,0,1:T(8,128)(2,1)} %copy.49), calls=%async_computation | async-start | bytes 19922944 | tf_op jit(solution)/shard_map/all_to_all | solution.py:57
  178.7 8.4 collective-permute-start.1
  204.1 2.3 copy-start
  262.2 18.4 %collective-permute-start = (f32[2,16,64,128]{3,2,1,0:T(8,128)}, f32[2,16,64,128]{3,2,1,0:T(8,128)S(1)}, u32[]{:S(2)}, u32[]{:S(2)}) collective-permute-start(f32[2,16,64,128]{3,2,1,0:T(8,128)} %get-tuple-element.355), channel_id=1, source_target_pairs={{0,4},{4,8},{8,12},{12,16},{16,20},{20,24},{24,28},{28,32},{32,36}... | collective-permute-start | bytes 3145736 | tf_op jit(solution)/shard_map/while/body/eval_jaxpr/ppermute | solution.py:17
  280.6 1.4 copy-start.1
  282.0 18.4 %collective-permute-start = (f32[2,16,64,128]{3,2,1,0:T(8,128)}, f32[2,16,64,128]{3,2,1,0:T(8,128)S(1)}, u32[]{:S(2)}, u32[]{:S(2)}) collective-permute-start(f32[2,16,64,128]{3,2,1,0:T(8,128)} %get-tuple-element.355), channel_id=1, source_target_pairs={{0,4},{4,8},{8,12},{12,16},{16,20},{20,24},{24,28},{28,32},{32,36}... | collective-permute-start | bytes 3145736 | tf_op jit(solution)/shard_map/while/body/eval_jaxpr/ppermute | solution.py:17
  300.4 1.4 copy-start.1
  301.8 18.4 %collective-permute-start = (f32[2,16,64,128]{3,2,1,0:T(8,128)}, f32[2,16,64,128]{3,2,1,0:T(8,128)S(1)}, u32[]{:S(2)}, u32[]{:S(2)}) collective-permute-start(f32[2,16,64,128]{3,2,1,0:T(8,128)} %get-tuple-element.355), channel_id=1, source_target_pairs={{0,4},{4,8},{8,12},{12,16},{16,20},{20,24},{24,28},{28,32},{32,36}... | collective-permute-start | bytes 3145736 | tf_op jit(solution)/shard_map/while/body/eval_jaxpr/ppermute | solution.py:17
  320.2 1.4 copy-start.1
  321.6 18.4 %collective-permute-start = (f32[2,16,64,128]{3,2,1,0:T(8,128)}, f32[2,16,64,128]{3,2,1,0:T(8,128)S(1)}, u32[]{:S(2)}, u32[]{:S(2)}) collective-permute-start(f32[2,16,64,128]{3,2,1,0:T(8,128)} %get-tuple-element.355), channel_id=1, source_target_pairs={{0,4},{4,8},{8,12},{12,16},{16,20},{20,24},{24,28},{28,32},{32,36}... | collective-permute-start | bytes 3145736 | tf_op jit(solution)/shard_map/while/body/eval_jaxpr/ppermute | solution.py:17
  340.0 1.4 copy-start.1
  341.4 18.4 %collective-permute-start = (f32[2,16,64,128]{3,2,1,0:T(8,128)}, f32[2,16,64,128]{3,2,1,0:T(8,128)S(1)}, u32[]{:S(2)}, u32[]{:S(2)}) collective-permute-start(f32[2,16,64,128]{3,2,1,0:T(8,128)} %get-tuple-element.355), channel_id=1, source_target_pairs={{0,4},{4,8},{8,12},{12,16},{16,20},{20,24},{24,28},{28,32},{32,36}... | collective-permute-start | bytes 3145736 | tf_op jit(solution)/shard_map/while/body/eval_jaxpr/ppermute | solution.py:17
  359.8 1.4 copy-start.1
  361.2 18.4 %collective-permute-start = (f32[2,16,64,128]{3,2,1,0:T(8,128)}, f32[2,16,64,128]{3,2,1,0:T(8,128)S(1)}, u32[]{:S(2)}, u32[]{:S(2)}) collective-permute-start(f32[2,16,64,128]{3,2,1,0:T(8,128)} %get-tuple-element.355), channel_id=1, source_target_pairs={{0,4},{4,8},{8,12},{12,16},{16,20},{20,24},{24,28},{28,32},{32,36}... | collective-permute-start | bytes 3145736 | tf_op jit(solution)/shard_map/while/body/eval_jaxpr/ppermute | solution.py:17
  379.6 1.4 copy-start.1
  381.0 18.4 %collective-permute-start = (f32[2,16,64,128]{3,2,1,0:T(8,128)}, f32[2,16,64,128]{3,2,1,0:T(8,128)S(1)}, u32[]{:S(2)}, u32[]{:S(2)}) collective-permute-start(f32[2,16,64,128]{3,2,1,0:T(8,128)} %get-tuple-element.355), channel_id=1, source_target_pairs={{0,4},{4,8},{8,12},{12,16},{16,20},{20,24},{24,28},{28,32},{32,36}... | collective-permute-start | bytes 3145736 | tf_op jit(solution)/shard_map/while/body/eval_jaxpr/ppermute | solution.py:17
  399.4 1.4 copy-start.1
  400.8 18.4 %collective-permute-start = (f32[2,16,64,128]{3,2,1,0:T(8,128)}, f32[2,16,64,128]{3,2,1,0:T(8,128)S(1)}, u32[]{:S(2)}, u32[]{:S(2)}) collective-permute-start(f32[2,16,64,128]{3,2,1,0:T(8,128)} %get-tuple-element.355), channel_id=1, source_target_pairs={{0,4},{4,8},{8,12},{12,16},{16,20},{20,24},{24,28},{28,32},{32,36}... | collective-permute-start | bytes 3145736 | tf_op jit(solution)/shard_map/while/body/eval_jaxpr/ppermute | solution.py:17
  420.5 18.4 %collective-permute-start = (f32[2,16,64,128]{3,2,1,0:T(8,128)}, f32[2,16,64,128]{3,2,1,0:T(8,128)S(1)}, u32[]{:S(2)}, u32[]{:S(2)}) collective-permute-start(f32[2,16,64,128]{3,2,1,0:T(8,128)} %get-tuple-element.355), channel_id=1, source_target_pairs={{0,4},{4,8},{8,12},{12,16},{16,20},{20,24},{24,28},{28,32},{32,36}... | collective-permute-start | bytes 3145736 | tf_op jit(solution)/shard_map/while/body/eval_jaxpr/ppermute | solution.py:17
  439.0 1.4 copy-start.1
  440.3 18.4 %collective-permute-start = (f32[2,16,64,128]{3,2,1,0:T(8,128)}, f32[2,16,64,128]{3,2,1,0:T(8,128)S(1)}, u32[]{:S(2)}, u32[]{:S(2)}) collective-permute-start(f32[2,16,64,128]{3,2,1,0:T(8,128)} %get-tuple-element.355), channel_id=1, source_target_pairs={{0,4},{4,8},{8,12},{12,16},{16,20},{20,24},{24,28},{28,32},{32,36}... | collective-permute-start | bytes 3145736 | tf_op jit(solution)/shard_map/while/body/eval_jaxpr/ppermute | solution.py:17
  458.8 1.4 copy-start.1
  460.1 18.4 %collective-permute-start = (f32[2,16,64,128]{3,2,1,0:T(8,128)}, f32[2,16,64,128]{3,2,1,0:T(8,128)S(1)}, u32[]{:S(2)}, u32[]{:S(2)}) collective-permute-start(f32[2,16,64,128]{3,2,1,0:T(8,128)} %get-tuple-element.355), channel_id=1, source_target_pairs={{0,4},{4,8},{8,12},{12,16},{16,20},{20,24},{24,28},{28,32},{32,36}... | collective-permute-start | bytes 3145736 | tf_op jit(solution)/shard_map/while/body/eval_jaxpr/ppermute | solution.py:17
  478.6 1.4 copy-start.1
  479.9 18.4 %collective-permute-start = (f32[2,16,64,128]{3,2,1,0:T(8,128)}, f32[2,16,64,128]{3,2,1,0:T(8,128)S(1)}, u32[]{:S(2)}, u32[]{:S(2)}) collective-permute-start(f32[2,16,64,128]{3,2,1,0:T(8,128)} %get-tuple-element.355), channel_id=1, source_target_pairs={{0,4},{4,8},{8,12},{12,16},{16,20},{20,24},{24,28},{28,32},{32,36}... | collective-permute-start | bytes 3145736 | tf_op jit(solution)/shard_map/while/body/eval_jaxpr/ppermute | solution.py:17
  498.4 1.4 copy-start.1
  499.7 18.4 %collective-permute-start = (f32[2,16,64,128]{3,2,1,0:T(8,128)}, f32[2,16,64,128]{3,2,1,0:T(8,128)S(1)}, u32[]{:S(2)}, u32[]{:S(2)}) collective-permute-start(f32[2,16,64,128]{3,2,1,0:T(8,128)} %get-tuple-element.355), channel_id=1, source_target_pairs={{0,4},{4,8},{8,12},{12,16},{16,20},{20,24},{24,28},{28,32},{32,36}... | collective-permute-start | bytes 3145736 | tf_op jit(solution)/shard_map/while/body/eval_jaxpr/ppermute | solution.py:17
  518.1 1.4 copy-start.1
  519.5 18.4 %collective-permute-start = (f32[2,16,64,128]{3,2,1,0:T(8,128)}, f32[2,16,64,128]{3,2,1,0:T(8,128)S(1)}, u32[]{:S(2)}, u32[]{:S(2)}) collective-permute-start(f32[2,16,64,128]{3,2,1,0:T(8,128)} %get-tuple-element.355), channel_id=1, source_target_pairs={{0,4},{4,8},{8,12},{12,16},{16,20},{20,24},{24,28},{28,32},{32,36}... | collective-permute-start | bytes 3145736 | tf_op jit(solution)/shard_map/while/body/eval_jaxpr/ppermute | solution.py:17
  537.9 1.4 copy-start.1
  539.3 18.4 %collective-permute-start = (f32[2,16,64,128]{3,2,1,0:T(8,128)}, f32[2,16,64,128]{3,2,1,0:T(8,128)S(1)}, u32[]{:S(2)}, u32[]{:S(2)}) collective-permute-start(f32[2,16,64,128]{3,2,1,0:T(8,128)} %get-tuple-element.355), channel_id=1, source_target_pairs={{0,4},{4,8},{8,12},{12,16},{16,20},{20,24},{24,28},{28,32},{32,36}... | collective-permute-start | bytes 3145736 | tf_op jit(solution)/shard_map/while/body/eval_jaxpr/ppermute | solution.py:17
  557.7 1.4 copy-start.1
  559.1 18.4 %collective-permute-start = (f32[2,16,64,128]{3,2,1,0:T(8,128)}, f32[2,16,64,128]{3,2,1,0:T(8,128)S(1)}, u32[]{:S(2)}, u32[]{:S(2)}) collective-permute-start(f32[2,16,64,128]{3,2,1,0:T(8,128)} %get-tuple-element.355), channel_id=1, source_target_pairs={{0,4},{4,8},{8,12},{12,16},{16,20},{20,24},{24,28},{28,32},{32,36}... | collective-permute-start | bytes 3145736 | tf_op jit(solution)/shard_map/while/body/eval_jaxpr/ppermute | solution.py:17
  577.5 1.4 copy-start.1
  578.9 18.4 %collective-permute-start = (f32[2,16,64,128]{3,2,1,0:T(8,128)}, f32[2,16,64,128]{3,2,1,0:T(8,128)S(1)}, u32[]{:S(2)}, u32[]{:S(2)}) collective-permute-start(f32[2,16,64,128]{3,2,1,0:T(8,128)} %get-tuple-element.355), channel_id=1, source_target_pairs={{0,4},{4,8},{8,12},{12,16},{16,20},{20,24},{24,28},{28,32},{32,36}... | collective-permute-start | bytes 3145736 | tf_op jit(solution)/shard_map/while/body/eval_jaxpr/ppermute | solution.py:17
  597.3 1.4 copy-start.1
  598.7 18.4 %collective-permute-start = (f32[2,16,64,128]{3,2,1,0:T(8,128)}, f32[2,16,64,128]{3,2,1,0:T(8,128)S(1)}, u32[]{:S(2)}, u32[]{:S(2)}) collective-permute-start(f32[2,16,64,128]{3,2,1,0:T(8,128)} %get-tuple-element.355), channel_id=1, source_target_pairs={{0,4},{4,8},{8,12},{12,16},{16,20},{20,24},{24,28},{28,32},{32,36}... | collective-permute-start | bytes 3145736 | tf_op jit(solution)/shard_map/while/body/eval_jaxpr/ppermute | solution.py:17
  617.1 1.4 copy-start.1
  618.5 18.4 %collective-permute-start = (f32[2,16,64,128]{3,2,1,0:T(8,128)}, f32[2,16,64,128]{3,2,1,0:T(8,128)S(1)}, u32[]{:S(2)}, u32[]{:S(2)}) collective-permute-start(f32[2,16,64,128]{3,2,1,0:T(8,128)} %get-tuple-element.355), channel_id=1, source_target_pairs={{0,4},{4,8},{8,12},{12,16},{16,20},{20,24},{24,28},{28,32},{32,36}... | collective-permute-start | bytes 3145736 | tf_op jit(solution)/shard_map/while/body/eval_jaxpr/ppermute | solution.py:17
  638.3 18.4 %collective-permute-start = (f32[2,16,64,128]{3,2,1,0:T(8,128)}, f32[2,16,64,128]{3,2,1,0:T(8,128)S(1)}, u32[]{:S(2)}, u32[]{:S(2)}) collective-permute-start(f32[2,16,64,128]{3,2,1,0:T(8,128)} %get-tuple-element.355), channel_id=1, source_target_pairs={{0,4},{4,8},{8,12},{12,16},{16,20},{20,24},{24,28},{28,32},{32,36}... | collective-permute-start | bytes 3145736 | tf_op jit(solution)/shard_map/while/body/eval_jaxpr/ppermute | solution.py:17
  656.7 1.4 copy-start.1
  658.1 18.4 %collective-permute-start = (f32[2,16,64,128]{3,2,1,0:T(8,128)}, f32[2,16,64,128]{3,2,1,0:T(8,128)S(1)}, u32[]{:S(2)}, u32[]{:S(2)}) collective-permute-start(f32[2,16,64,128]{3,2,1,0:T(8,128)} %get-tuple-element.355), channel_id=1, source_target_pairs={{0,4},{4,8},{8,12},{12,16},{16,20},{20,24},{24,28},{28,32},{32,36}... | collective-permute-start | bytes 3145736 | tf_op jit(solution)/shard_map/while/body/eval_jaxpr/ppermute | solution.py:17
  677.9 18.4 %collective-permute-start = (f32[2,16,64,128]{3,2,1,0:T(8,128)}, f32[2,16,64,128]{3,2,1,0:T(8,128)S(1)}, u32[]{:S(2)}, u32[]{:S(2)}) collective-permute-start(f32[2,16,64,128]{3,2,1,0:T(8,128)} %get-tuple-element.355), channel_id=1, source_target_pairs={{0,4},{4,8},{8,12},{12,16},{16,20},{20,24},{24,28},{28,32},{32,36}... | collective-permute-start | bytes 3145736 | tf_op jit(solution)/shard_map/while/body/eval_jaxpr/ppermute | solution.py:17
  696.3 1.4 copy-start.1
  697.7 18.4 %collective-permute-start = (f32[2,16,64,128]{3,2,1,0:T(8,128)}, f32[2,16,64,128]{3,2,1,0:T(8,128)S(1)}, u32[]{:S(2)}, u32[]{:S(2)}) collective-permute-start(f32[2,16,64,128]{3,2,1,0:T(8,128)} %get-tuple-element.355), channel_id=1, source_target_pairs={{0,4},{4,8},{8,12},{12,16},{16,20},{20,24},{24,28},{28,32},{32,36}... | collective-permute-start | bytes 3145736 | tf_op jit(solution)/shard_map/while/body/eval_jaxpr/ppermute | solution.py:17
  717.5 18.4 %collective-permute-start = (f32[2,16,64,128]{3,2,1,0:T(8,128)}, f32[2,16,64,128]{3,2,1,0:T(8,128)S(1)}, u32[]{:S(2)}, u32[]{:S(2)}) collective-permute-start(f32[2,16,64,128]{3,2,1,0:T(8,128)} %get-tuple-element.355), channel_id=1, source_target_pairs={{0,4},{4,8},{8,12},{12,16},{16,20},{20,24},{24,28},{28,32},{32,36}... | collective-permute-start | bytes 3145736 | tf_op jit(solution)/shard_map/while/body/eval_jaxpr/ppermute | solution.py:17
  735.9 1.4 copy-start.1
  737.3 18.4 %collective-permute-start = (f32[2,16,64,128]{3,2,1,0:T(8,128)}, f32[2,16,64,128]{3,2,1,0:T(8,128)S(1)}, u32[]{:S(2)}, u32[]{:S(2)}) collective-permute-start(f32[2,16,64,128]{3,2,1,0:T(8,128)} %get-tuple-element.355), channel_id=1, source_target_pairs={{0,4},{4,8},{8,12},{12,16},{16,20},{20,24},{24,28},{28,32},{32,36}... | collective-permute-start | bytes 3145736 | tf_op jit(solution)/shard_map/while/body/eval_jaxpr/ppermute | solution.py:17
  757.0 18.4 %collective-permute-start = (f32[2,16,64,128]{3,2,1,0:T(8,128)}, f32[2,16,64,128]{3,2,1,0:T(8,128)S(1)}, u32[]{:S(2)}, u32[]{:S(2)}) collective-permute-start(f32[2,16,64,128]{3,2,1,0:T(8,128)} %get-tuple-element.355), channel_id=1, source_target_pairs={{0,4},{4,8},{8,12},{12,16},{16,20},{20,24},{24,28},{28,32},{32,36}... | collective-permute-start | bytes 3145736 | tf_op jit(solution)/shard_map/while/body/eval_jaxpr/ppermute | solution.py:17
  775.5 1.4 copy-start.1
  776.8 18.4 %collective-permute-start = (f32[2,16,64,128]{3,2,1,0:T(8,128)}, f32[2,16,64,128]{3,2,1,0:T(8,128)S(1)}, u32[]{:S(2)}, u32[]{:S(2)}) collective-permute-start(f32[2,16,64,128]{3,2,1,0:T(8,128)} %get-tuple-element.355), channel_id=1, source_target_pairs={{0,4},{4,8},{8,12},{12,16},{16,20},{20,24},{24,28},{28,32},{32,36}... | collective-permute-start | bytes 3145736 | tf_op jit(solution)/shard_map/while/body/eval_jaxpr/ppermute | solution.py:17
  796.6 18.4 %collective-permute-start = (f32[2,16,64,128]{3,2,1,0:T(8,128)}, f32[2,16,64,128]{3,2,1,0:T(8,128)S(1)}, u32[]{:S(2)}, u32[]{:S(2)}) collective-permute-start(f32[2,16,64,128]{3,2,1,0:T(8,128)} %get-tuple-element.355), channel_id=1, source_target_pairs={{0,4},{4,8},{8,12},{12,16},{16,20},{20,24},{24,28},{28,32},{32,36}... | collective-permute-start | bytes 3145736 | tf_op jit(solution)/shard_map/while/body/eval_jaxpr/ppermute | solution.py:17
  815.1 1.4 copy-start.1
  816.4 18.4 %collective-permute-start = (f32[2,16,64,128]{3,2,1,0:T(8,128)}, f32[2,16,64,128]{3,2,1,0:T(8,128)S(1)}, u32[]{:S(2)}, u32[]{:S(2)}) collective-permute-start(f32[2,16,64,128]{3,2,1,0:T(8,128)} %get-tuple-element.355), channel_id=1, source_target_pairs={{0,4},{4,8},{8,12},{12,16},{16,20},{20,24},{24,28},{28,32},{32,36}... | collective-permute-start | bytes 3145736 | tf_op jit(solution)/shard_map/while/body/eval_jaxpr/ppermute | solution.py:17
  834.9 1.4 copy-start.1
  836.2 18.4 %collective-permute-start = (f32[2,16,64,128]{3,2,1,0:T(8,128)}, f32[2,16,64,128]{3,2,1,0:T(8,128)S(1)}, u32[]{:S(2)}, u32[]{:S(2)}) collective-permute-start(f32[2,16,64,128]{3,2,1,0:T(8,128)} %get-tuple-element.355), channel_id=1, source_target_pairs={{0,4},{4,8},{8,12},{12,16},{16,20},{20,24},{24,28},{28,32},{32,36}... | collective-permute-start | bytes 3145736 | tf_op jit(solution)/shard_map/while/body/eval_jaxpr/ppermute | solution.py:17
  854.6 1.4 copy-start.1
  856.0 18.4 %collective-permute-start = (f32[2,16,64,128]{3,2,1,0:T(8,128)}, f32[2,16,64,128]{3,2,1,0:T(8,128)S(1)}, u32[]{:S(2)}, u32[]{:S(2)}) collective-permute-start(f32[2,16,64,128]{3,2,1,0:T(8,128)} %get-tuple-element.355), channel_id=1, source_target_pairs={{0,4},{4,8},{8,12},{12,16},{16,20},{20,24},{24,28},{28,32},{32,36}... | collective-permute-start | bytes 3145736 | tf_op jit(solution)/shard_map/while/body/eval_jaxpr/ppermute | solution.py:17
  874.4 1.4 copy-start.1
  (6 other events, 8.2 us)
where the time goes:
time: 941 us; the launch traced here: 930 us
  waiting for transfers between devices  635 us (67%)
  local copies, waits for them, and re-layouts  106 us (11%)
  other arithmetic  80.1 us (9%)
  starting transfers between devices  68.7 us (7%)
  matrix products  38.6 us (4%)
    ppermute x32, waiting for transfers between devices, passed_along(): return lax.ppermute(shard, axis, pairs)  512 us
    all_to_all x1, waiting for transfers between devices, per_device(): lax.all_to_all(projected, 'seq', split_axis=1, concat_axis=0, tiled=True)  123 us
    ppermute x32, starting transfers between devices, passed_along(): return lax.ppermute(shard, axis, pairs)  61.1 us
    add x31, other arithmetic, relay_step(): return (received, device_decay[..., None, None] * received + device_state)  41.8 us
    all_to_all x3, local copies, waits for them, and re-layouts, per_device(): lax.all_to_all(projected, 'seq', split_axis=1, concat_axis=0, tiled=True)  31.3 us
    unnamed x15, local copies, waits for them, and re-layouts  22.5 us
  transfers between devices with their start and end apart: 33, of which 32 were waited for; matrix products, arithmetic and copies ran while one was open for 1% of the time, Pallas kernels for 0%

commit v1 on v0

v1 whole, which is shorter than its diff:
```python
import functools

import jax
import jax.numpy as jnp
from jax import lax
from jax.experimental import pallas as pl
from jax.experimental.pallas import tpu as pltpu
from jax.sharding import PartitionSpec as P

MESH = pl.DeviceIdType.MESH
HEAD_DIM = 64
STATE_WIDTH = 128
CHUNK = 128
CHUNKS = 8
GROUPS = 2
HEADS = 16
SPAN = HEADS * HEAD_DIM
CONV = SPAN + 2 * STATE_WIDTH
COLS = SPAN + CONV + HEADS
EPSILON = 1e-05

F32 = jnp.float32
BF16 = jnp.bfloat16


def silu(v):
    return v * (1.0 / (1.0 + jnp.exp(-v)))


def dot(a, b, precision=None):
    return jnp.dot(a, b, preferred_element_type=F32, precision=precision)


def kernel(
    n, x_ref, conv_ref, par_ref, gain_ref, out_ref,
    recv, rows, taps, prev, act, wgt, state, ys, gate, outmap, reach, lead, bmat,
    halo_out, halo_in, own, gathered, prefix, incoming, fade_out, fade_in, staged,
    chunk_send, chunk_recv, chunk_own, halo_send, halo_recv,
    scan_send, scan_recv, fade_send, fade_recv, back_send, back_recv, out_sem,
):
    me = lax.axis_index("seq")
    slab = COLS * GROUPS // n
    per_group = n // GROUPS
    per_device = GROUPS * HEADS // n

    barrier = pltpu.get_barrier_semaphore()

    def greet(i, _):
        pl.semaphore_signal(
            barrier, inc=1, device_id={"seq": lax.rem(me + i, n)}, device_id_type=MESH
        )
        return 0

    lax.fori_loop(1, n, greet, 0)
    pl.semaphore_wait(barrier, n - 1)

    def piece(device, c):
        first = pl.multiple_of(device * (CHUNK * CHUNKS) + c * CHUNK, CHUNK)
        return x_ref.at[:, pl.ds(first, CHUNK)]

    def send_chunk(turn, _):
        c = lax.rem(turn + CHUNKS - 1, CHUNKS)
        pltpu.make_async_copy(piece(me, c), recv.at[c, me], chunk_own.at[c]).start()

        def send(i, _):
            device = lax.rem(me + i, n)
            pltpu.make_async_remote_copy(
                src_ref=piece(device, c),
                dst_ref=recv.at[c, me],
                send_sem=chunk_send.at[c],
                recv_sem=chunk_recv.at[c],
                device_id={"seq": device},
                device_id_type=MESH,
            ).start()
            return 0

        lax.fori_loop(1, n, send, 0)
        return 0

    lax.fori_loop(0, CHUNKS, send_chunk, 0)

    def wait_chunk(c):
        peers = recv.at[c, pl.ds(0, n - 1)]
        pltpu.make_async_copy(peers, peers, chunk_recv.at[c]).wait()
        pltpu.make_async_copy(recv.at[c, 0], recv.at[c, 0], chunk_own.at[c]).wait()

    sub = lax.broadcasted_iota(jnp.int32, (CHUNK, CHUNK), 0)
    lane = lax.broadcasted_iota(jnp.int32, (CHUNK, CHUNK), 1)
    causal = sub <= lane

    for g in range(GROUPS):
        for i in range(CONV // CHUNK):
            four = jnp.concatenate(
                [conv_ref[k, g : g + 1, i * CHUNK : (i + 1) * CHUNK] for k in range(4)]
                + [jnp.zeros((CHUNK - 4, CHUNK), F32)],
                axis=0,
            )
            turned = jnp.transpose(four)
            for k in range(4):
                taps[g, k, i * CHUNK : (i + 1) * CHUNK, :] = jnp.broadcast_to(
                    turned[:, k : k + 1], (CHUNK, CHUNK)
                )
    lead[...] = jnp.zeros_like(lead)
    state[...] = jnp.zeros_like(state)

    def lay_out(c, g):
        for k in range(per_group):
            rows[k * slab : (k + 1) * slab, :] = recv[c, g * per_group + k].astype(F32)

    wait_chunk(CHUNKS - 1)

    def make_halo(g, _):
        lay_out(CHUNKS - 1, g)
        for i in range(CONV // CHUNK):
            tile = rows[SPAN + i * CHUNK : SPAN + (i + 1) * CHUNK, :]
            halo_out[g, :, i * CHUNK : (i + 1) * CHUNK] = jnp.transpose(tile)[CHUNK - 8 :, :]
        return 0

    lax.fori_loop(0, GROUPS, make_halo, 0)
    halo_copy = pltpu.make_async_remote_copy(
        src_ref=halo_out,
        dst_ref=halo_in,
        send_sem=halo_send,
        recv_sem=halo_recv,
        device_id={"seq": lax.rem(me + 1, n)},
        device_id_type=MESH,
    )
    halo_copy.start()
    halo_copy.wait()
    has_past = jnp.where(me > 0, 1.0, 0.0).astype(F32)
    for g in range(GROUPS):
        for i in range(CONV // CHUNK):
            tail = halo_in[g, :, i * CHUNK : (i + 1) * CHUNK] * has_past
            tile = jnp.concatenate([jnp.zeros((CHUNK - 8, CHUNK), F32), tail], axis=0)
            prev[g, i * CHUNK : (i + 1) * CHUNK, :] = jnp.transpose(tile)

    def unit(u, _):
        c = u // GROUPS
        g = lax.rem(u, GROUPS)

        @pl.when(jnp.logical_and(g == 0, c < CHUNKS - 1))
        def _():
            wait_chunk(c)

        lay_out(c, g)
        for i in range(SPAN // CHUNK):
            gate[u, i * CHUNK : (i + 1) * CHUNK, :] = silu(rows[i * CHUNK : (i + 1) * CHUNK, :])
        for i in range(CONV // CHUNK):
            span = slice(i * CHUNK, (i + 1) * CHUNK)
            current = rows[SPAN + i * CHUNK : SPAN + (i + 1) * CHUNK, :]
            past = prev[g, span, :]
            total = taps[g, 3, span, :] * current
            for k in range(1, 4):
                shifted = pltpu.roll(jnp.where(lane >= CHUNK - k, past, current), k, 1)
                total += taps[g, 3 - k, span, :] * shifted
            prev[g, span, :] = current
            value = silu(total)
            if i < SPAN // CHUNK:
                act[span, :] = value.astype(BF16)
            elif i == SPAN // CHUNK:
                bmat[...] = jnp.transpose(value).astype(BF16)
            else:
                outmap[u] = value.astype(BF16)

        raw = rows[SPAN + CONV :, :] + par_ref[0, g]
        step = jnp.maximum(raw, 0.0) + jnp.log1p(jnp.exp(-jnp.abs(raw)))
        log_decay = -jnp.exp(par_ref[1, g]) * step
        running = dot(log_decay, causal.astype(F32), lax.Precision.HIGHEST)
        last = jnp.broadcast_to(running[:, CHUNK - 1 :], (HEADS, CHUNK))
        since = jnp.exp(running)
        until = jnp.exp(last - running) * step
        fade = jnp.exp(last)
        reach[u] = jnp.exp(running + lead[g])
        lead[g] += last
        columns = jnp.transpose(
            jnp.concatenate(
                [running - jnp.log(step), jnp.zeros((CHUNK - HEADS, CHUNK), F32)], axis=0
            )
        )
        cmat = outmap[u]
        scores = dot(bmat[...], cmat)
        high = state[g].astype(BF16)
        low = (state[g] - high.astype(F32)).astype(BF16)
        carried = dot(
            jnp.concatenate([high, low], axis=1), jnp.concatenate([cmat, cmat], axis=0)
        )
        ys[u] = carried
        for h in range(HEADS):
            span = slice(h * HEAD_DIM, (h + 1) * HEAD_DIM)
            gaps = running[h : h + 1, :] - columns[:, h : h + 1]
            weights = (scores * jnp.exp(jnp.where(causal, gaps, -jnp.inf))).astype(BF16)
            x = act[span, :]
            wide = x.astype(F32)
            ys[u, span, :] = (
                dot(x, weights)
                + par_ref[2, g, h : h + 1, :] * wide
                + ys[u, span, :] * since[h : h + 1, :]
            )
            wgt[span, :] = (wide * until[h : h + 1, :]).astype(BF16)
        update = dot(wgt[...], bmat[...])
        for h in range(HEADS):
            span = slice(h * HEAD_DIM, (h + 1) * HEAD_DIM)
            state[g, span, :] = state[g, span, :] * fade[h : h + 1, :] + update[span, :]
        return 0

    lax.fori_loop(0, CHUNKS * GROUPS, unit, 0)

    for g in range(GROUPS):
        own[g * SPAN : (g + 1) * SPAN, :] = state[g].astype(BF16)
        for h in range(HEADS):
            first = (g * HEADS + h) * 8
            fade_out[first : first + 8, :] = jnp.broadcast_to(
                jnp.exp(lead[g, h : h + 1, :]), (8, CHUNK)
            )

    def heads_of(ref, device, height):
        size = per_device * height
        return ref.at[pl.ds(pl.multiple_of(device * size, size), size)]

    def send_states(i, _):
        device = lax.rem(me + i, n)
        for source, target, send_sem, recv_sem, height in (
            (own, gathered, scan_send, scan_recv, HEAD_DIM),
            (fade_out, fade_in, fade_send, fade_recv, 8),
        ):
            pltpu.make_async_remote_copy(
                src_ref=heads_of(source, device, height),
                dst_ref=heads_of(target, me, height),
                send_sem=send_sem,
                recv_sem=recv_sem,
                device_id={"seq": device},
                device_id_type=MESH,
            ).start()
        return 0

    lax.fori_loop(1, n, send_states, 0)
    heads_of(gathered, me, HEAD_DIM)[...] = heads_of(own, me, HEAD_DIM)[...]
    heads_of(fade_in, me, 8)[...] = heads_of(fade_out, me, 8)[...]

    def wait_all(ref, sem, height):
        peers = ref.at[pl.ds(0, (n - 1) * per_device * height)]
        pltpu.make_async_copy(peers, peers, sem).wait()

    wait_all(gathered, scan_recv, HEAD_DIM)
    wait_all(fade_in, fade_recv, 8)

    def horner(device, reached):
        heads_of(prefix, device, HEAD_DIM)[...] = reached.reshape(
            per_device * HEAD_DIM, STATE_WIDTH
        ).astype(BF16)
        factor = heads_of(fade_in, device, 8)[...].reshape(per_device, 1, 8, STATE_WIDTH)
        added = heads_of(gathered, device, HEAD_DIM)[...].astype(F32)
        return reached * factor + added.reshape(per_device, 8, 8, STATE_WIDTH)

    lax.fori_loop(0, n, horner, jnp.zeros((per_device, 8, 8, STATE_WIDTH), F32))

    def send_back(i, _):
        device = lax.rem(me + i, n)
        pltpu.make_async_remote_copy(
            src_ref=heads_of(prefix, device, HEAD_DIM),
            dst_ref=heads_of(incoming, me, HEAD_DIM),
            send_sem=back_send,
            recv_sem=back_recv,
            device_id={"seq": device},
            device_id_type=MESH,
        ).start()
        return 0

    lax.fori_loop(1, n, send_back, 0)
    heads_of(incoming, me, HEAD_DIM)[...] = heads_of(prefix, me, HEAD_DIM)[...]
    wait_all(incoming, back_recv, HEAD_DIM)

    def finish(u, _):
        c = u // GROUPS
        g = lax.rem(u, GROUPS)
        arrived = dot(
            incoming[pl.ds(pl.multiple_of(g * SPAN, SPAN), SPAN), :], outmap[u]
        )
        squares = jnp.zeros((1, CHUNK), F32)
        for h in range(HEADS):
            span = slice(h * HEAD_DIM, (h + 1) * HEAD_DIM)
            mixed = ys[u, span, :] + arrived[span, :] * reach[u, h : h + 1, :]
            gated = mixed * gate[u, span, :]
            ys[u, span, :] = gated
            squares += jnp.sum(gated * gated, axis=0, keepdims=True)
        scale = lax.rsqrt(squares * (1.0 / SPAN) + EPSILON)
        for i in range(SPAN // CHUNK):
            span = slice(i * CHUNK, (i + 1) * CHUNK)
            turned = jnp.transpose(ys[u, span, :] * scale)
            staged[u, :, span] = (turned * gain_ref[g, :, span]).astype(BF16)
        pltpu.make_async_copy(
            staged.at[u],
            out_ref.at[
                pl.ds(pl.multiple_of(c * CHUNK, CHUNK), CHUNK),
                pl.ds(pl.multiple_of(g * SPAN, SPAN), SPAN),
            ],
            out_sem,
        ).start()
        return 0

    lax.fori_loop(0, CHUNKS * GROUPS, finish, 0)

    def drain(c, _):
        peers = recv.at[c, pl.ds(0, n - 1)]
        pltpu.make_async_copy(peers, peers, chunk_send.at[c]).wait()
        return 0

    lax.fori_loop(0, CHUNKS, drain, 0)
    wait_all(own, scan_send, HEAD_DIM)
    wait_all(fade_out, fade_send, 8)
    wait_all(prefix, back_send, HEAD_DIM)
    pltpu.make_async_copy(staged, staged, out_sem).wait()


def per_device(projected, conv_weight, dt_bias, a_log, d_skip, norm_gain):
    n = lax.axis_size("seq")
    slab = COLS * GROUPS // n
    tokens = CHUNK * CHUNKS
    units = GROUPS * CHUNKS
    heads = GROUPS * HEADS
    params = jnp.broadcast_to(
        jnp.stack([dt_bias, a_log, d_skip]).reshape(3, GROUPS, HEADS, 1),
        (3, GROUPS, HEADS, CHUNK),
    )
    gain = norm_gain.reshape(GROUPS, 1, SPAN)
    vmem = pl.BlockSpec(memory_space=pltpu.VMEM)
    anywhere = pl.BlockSpec(memory_space=pl.ANY)
    dma = pltpu.SemaphoreType.DMA
    return pl.pallas_call(
        functools.partial(kernel, n),
        out_shape=jax.ShapeDtypeStruct((tokens, GROUPS * SPAN), BF16),
        in_specs=[anywhere, vmem, vmem, vmem],
        out_specs=anywhere,
        scratch_shapes=[
            pltpu.VMEM((CHUNKS, n, slab, CHUNK), BF16),
            pltpu.VMEM((COLS, CHUNK), F32),
            pltpu.VMEM((GROUPS, 4, CONV, CHUNK), F32),
            pltpu.VMEM((GROUPS, CONV, CHUNK), F32),
            pltpu.VMEM((SPAN, CHUNK), BF16),
            pltpu.VMEM((SPAN, CHUNK), BF16),
            pltpu.VMEM((GROUPS, SPAN, STATE_WIDTH), F32),
            pltpu.VMEM((units, SPAN, CHUNK), F32),
            pltpu.VMEM((units, SPAN, CHUNK), F32),
            pltpu.VMEM((units, STATE_WIDTH, CHUNK), BF16),
            pltpu.VMEM((units, HEADS, CHUNK), F32),
            pltpu.VMEM((GROUPS, HEADS, CHUNK), F32),
            pltpu.VMEM((CHUNK, STATE_WIDTH), BF16),
            pltpu.VMEM((GROUPS, 8, CONV), F32),
            pltpu.VMEM((GROUPS, 8, CONV), F32),
            pltpu.VMEM((heads * HEAD_DIM, STATE_WIDTH), BF16),
            pltpu.VMEM((heads * HEAD_DIM, STATE_WIDTH), BF16),
            pltpu.VMEM((heads * HEAD_DIM, STATE_WIDTH), BF16),
            pltpu.VMEM((heads * HEAD_DIM, STATE_WIDTH), BF16),
            pltpu.VMEM((heads * 8, STATE_WIDTH), F32),
            pltpu.VMEM((heads * 8, STATE_WIDTH), F32),
            pltpu.VMEM((units, CHUNK, SPAN), BF16),
            dma((CHUNKS,)), dma((CHUNKS,)), dma((CHUNKS,)), dma, dma,
            dma, dma, dma, dma, dma, dma, dma,
        ],
        compiler_params=pltpu.CompilerParams(
            collective_id=0, has_side_effects=True, vmem_limit_bytes=58 * 2**20
        ),
    )(projected, conv_weight, params, gain)


def solution(mesh):
    in_specs = (P(("tp", "seq"), None), P(None, "tp", None), P("tp"), P("tp"), P("tp"), P("tp"))
    return jax.shard_map(
        per_device, mesh=mesh, in_specs=in_specs, out_specs=P("seq", "tp"), check_vma=False
    )
```

time: 941 us -> 179 us (0.19)
  the two profiles are of different devices: /device:TPU:112 before, /device:TPU:1 now
where the time goes in v1:
time: 179 us
  Pallas kernels  171 us (96%)
  local copies, waits for them, and re-layouts  7.69 us (4%)
    pallas_call x1, Pallas kernels, per_device(): pl.pallas_call(functools.partial(kernel, n), out_shape=jax.ShapeDtypeStru...  171 us
    unnamed x1, local copies, waits for them, and re-layouts  4.79 us

profile of v1, /device:TPU:1, one launch (start us, length us, event | category | flops | bytes accessed | tf_op | source)
XLA Modules:
  0.0 178.8 jit_solution(17320869378714399458)
XLA Ops:
  0.0 0.7 stack.12
  0.7 0.7 stack.13
  1.5 0.7 stack.14
  2.2 0.7 broadcast_in_dim.8.par_ref
  2.9 171.1 %shard_map.64 = bf16[1024,2048]{1,0:T(8,128)(2,1)} custom-call(bf16[145,32768]{1,0:T(8,128)(2,1)} %x_ref.1, f32[4,2,1280]{2,1,0:T(2,128)} %conv_ref.1, f32[3,2,16,128]{3,2,1,0:T(8,128)} %broadcast_in_dim.8.par_ref, f32[2,1,1024]{2,1,0:T(1,128)} %bitcast.3), custom_call_target="tpu_custom_call" | custom-call | tf_op jit(solution)/shard_map/pallas_call | solution.py:329
  174.0 4.8 %copy.8 = bf16[1024,2048]{1,0:T(8,128)(2,1)} copy(bf16[1024,2048]{1,0:T(8,128)(2,1)} %shard_map.64) | data formatting | bytes 8388608
  (1 shorter events, 0.0 us)

commit v2 on v1

v2 whole, which is shorter than its diff:
```python
import functools

import jax
import jax.numpy as jnp
from jax import lax
from jax.experimental import pallas as pl
from jax.experimental.pallas import tpu as pltpu
from jax.sharding import PartitionSpec as P

MESH = pl.DeviceIdType.MESH
HEAD_DIM = 64
STATE_WIDTH = 128
CHUNK = 128
CHUNKS = 8
GROUPS = 2
HEADS = 16
SPAN = HEADS * HEAD_DIM
CONV = SPAN + 2 * STATE_WIDTH
COLS = SPAN + CONV + HEADS
EPSILON = 1e-05
AHEAD = 3
HELD = 4
MESSAGE = HEAD_DIM + 16

F32 = jnp.float32
BF16 = jnp.bfloat16


def silu(v):
    return v * (1.0 / (1.0 + jnp.exp(-v)))


def dot(a, b, precision=None):
    return jnp.dot(a, b, preferred_element_type=F32, precision=precision)


def dot_nt(a, b):
    return lax.dot_general(a, b, (((1,), (1,)), ((), ())), preferred_element_type=F32)


def kernel(
    n, x_ref, conv_hbm, bias_hbm, rate_hbm, skip_hbm, gain_hbm, out_ref,
    conv_ref, bias_ref, rate_ref, skip_ref, gain_ref, recv, rows, gates, taps, params, prev, act, wgt, state, carried, within, into,
    outmap, outrows, small, lead, turned_gate, turned_own,
    halo_out, halo_in, own, gathered, prefix, incoming, staged,
    chunk_send, chunk_recv, chunk_own, halo_send, halo_recv,
    scan_send, scan_recv, back_send, back_recv, out_sem, small_sem,
):
    me = lax.axis_index("seq")
    slab = COLS * GROUPS // n
    per_group = n // GROUPS
    per_device = GROUPS * HEADS // n

    loads = [
        pltpu.make_async_copy(source, target, small_sem.at[k])
        for k, (source, target) in enumerate(
            (
                (conv_hbm, conv_ref),
                (bias_hbm, bias_ref),
                (rate_hbm, rate_ref),
                (skip_hbm, skip_ref),
                (gain_hbm, gain_ref),
            )
        )
    ]
    for load in loads:
        load.start()

    barrier = pltpu.get_barrier_semaphore()

    def greet(i, _):
        pl.semaphore_signal(
            barrier, inc=1, device_id={"seq": lax.rem(me + i, n)}, device_id_type=MESH
        )
        return 0

    lax.fori_loop(1, n, greet, 0)
    pl.semaphore_wait(barrier, n - 1)

    def peer(i, shift):
        move = lax.rem(i * 11 + shift, n - 1) + 1
        if n != 32:
            return lax.rem(me + move, n)
        y = lax.rem(me // 8 + move // 8, 4)
        x = lax.rem(me // 2 + move // 2, 4)
        core = lax.rem(me + move, 2)
        return y * 8 + x * 2 + core

    def piece(device, c):
        first = pl.multiple_of(device * (CHUNK * CHUNKS) + c * CHUNK, CHUNK)
        return x_ref.at[:, pl.ds(first, CHUNK)]

    def send_chunk(turn, _):
        c = lax.rem(turn + CHUNKS - 1, CHUNKS)

        def send(i, _):
            device = peer(i, c * 5)
            pltpu.make_async_remote_copy(
                src_ref=piece(device, c),
                dst_ref=recv.at[c, me],
                send_sem=chunk_send.at[c],
                recv_sem=chunk_recv.at[c],
                device_id={"seq": device},
                device_id_type=MESH,
            ).start()
            return 0

        lax.fori_loop(0, n - 1, send, 0)
        pltpu.make_async_copy(piece(me, c), recv.at[c, me], chunk_own.at[c]).start()
        return 0

    lax.fori_loop(0, AHEAD, send_chunk, 0)

    def wait_chunk(c):
        peers = recv.at[c, pl.ds(0, n - 1)]
        pltpu.make_async_copy(peers, peers, chunk_recv.at[c]).wait()
        pltpu.make_async_copy(recv.at[c, 0], recv.at[c, 0], chunk_own.at[c]).wait()

    sub = lax.broadcasted_iota(jnp.int32, (CHUNK, CHUNK), 0)
    lane = lax.broadcasted_iota(jnp.int32, (CHUNK, CHUNK), 1)
    causal = sub <= lane

    for load in loads:
        load.wait()

    def taps_of(g, i):
        four = jnp.concatenate(
            [conv_ref[k, g : g + 1, i * CHUNK : (i + 1) * CHUNK] for k in range(4)]
            + [jnp.zeros((CHUNK - 4, CHUNK), F32)],
            axis=0,
        )
        turned = jnp.transpose(four)
        for k in range(4):
            taps[g, k, i * CHUNK : (i + 1) * CHUNK, :] = jnp.broadcast_to(
                turned[:, k : k + 1], (CHUNK, CHUNK)
            )

    for g in range(GROUPS):
        for i in range(CONV // CHUNK):
            taps_of(g, i)
    rows[0:CHUNK, :] = jnp.zeros((CHUNK, CHUNK), F32)
    for k, ref in enumerate((bias_ref, rate_ref, skip_ref)):
        rows[k : k + 1, 0 : GROUPS * HEADS] = ref[...]
    turned = jnp.transpose(rows[0:CHUNK, :])
    for k in range(3):
        for g in range(GROUPS):
            params[k, g] = jnp.broadcast_to(
                turned[g * HEADS : (g + 1) * HEADS, k : k + 1], (HEADS, CHUNK)
            )
    lead[...] = jnp.zeros_like(lead)
    state[...] = jnp.zeros_like(state)

    def lay_out(c, g):
        for k in range(SPAN // slab, per_group):
            rows[k * slab : (k + 1) * slab, :] = recv[c, g * per_group + k].astype(F32)

    def lay_out_gates(c, g):
        for k in range(-(-SPAN // slab)):
            gates[k * slab : (k + 1) * slab, :] = recv[c, g * per_group + k].astype(F32)

    wait_chunk(CHUNKS - 1)
    send_chunk(AHEAD, 0)

    def make_halo(g, _):
        lay_out(CHUNKS - 1, g)
        for i in range(CONV // CHUNK):
            tile = rows[SPAN + i * CHUNK : SPAN + (i + 1) * CHUNK, :]
            halo_out[g, :, i * CHUNK : (i + 1) * CHUNK] = jnp.transpose(tile)[CHUNK - 8 :, :]
        return 0

    lax.fori_loop(0, GROUPS, make_halo, 0)
    halo_copy = pltpu.make_async_remote_copy(
        src_ref=halo_out,
        dst_ref=halo_in,
        send_sem=halo_send,
        recv_sem=halo_recv,
        device_id={"seq": lax.rem(me + 1, n)},
        device_id_type=MESH,
    )
    halo_copy.start()
    halo_copy.wait()
    has_past = jnp.where(me > 0, 1.0, 0.0).astype(F32)
    for g in range(GROUPS):
        for i in range(CONV // CHUNK):
            tail = halo_in[g, :, i * CHUNK : (i + 1) * CHUNK] * has_past
            tile = jnp.concatenate([jnp.zeros((CHUNK - 8, CHUNK), F32), tail], axis=0)
            prev[g, i * CHUNK : (i + 1) * CHUNK, :] = jnp.transpose(tile)

    def advance(u, _):
        c = u // GROUPS
        g = lax.rem(u, GROUPS)
        slot = lax.rem(u, HELD)

        @pl.when(jnp.logical_and(g == 0, c < CHUNKS - 1))
        def _():
            wait_chunk(c)

            @pl.when(c + 1 + AHEAD < CHUNKS)
            def _():
                send_chunk(c + 1 + AHEAD, 0)

        lay_out(c, g)
        for i in range(CONV // CHUNK):
            span = slice(i * CHUNK, (i + 1) * CHUNK)
            current = rows[SPAN + i * CHUNK : SPAN + (i + 1) * CHUNK, :]
            past = prev[g, span, :]
            total = taps[g, 3, span, :] * current
            for k in range(1, 4):
                shifted = pltpu.roll(jnp.where(lane >= CHUNK - k, past, current), k, 1)
                total += taps[g, 3 - k, span, :] * shifted
            prev[g, span, :] = current
            value = silu(total)
            if i < SPAN // CHUNK:
                act[slot, span, :] = value.astype(BF16)
            elif i == SPAN // CHUNK:
                into[slot] = jnp.transpose(value).astype(BF16)
            else:
                outmap[slot] = value.astype(BF16)
                outrows[u] = jnp.transpose(value).astype(BF16)

        raw = rows[SPAN + CONV : COLS, :] + params[0, g]
        step = jnp.maximum(raw, 0.0) + jnp.log1p(jnp.exp(-jnp.abs(raw)))
        log_decay = -jnp.exp(params[1, g]) * step
        running = dot(log_decay, causal.astype(F32), lax.Precision.HIGHEST)
        last = jnp.broadcast_to(running[:, CHUNK - 1 :], (HEADS, CHUNK))
        until = jnp.exp(last - running) * step
        fade = jnp.exp(last)
        small[slot, 0] = running
        small[slot, 1] = jnp.exp(running)
        small[slot, 2] = jnp.exp(running + lead[g])
        lead[g] += last
        within[slot] = jnp.transpose(
            jnp.concatenate(
                [running - jnp.log(step), jnp.zeros((CHUNK - HEADS, CHUNK), F32)], axis=0
            )
        )
        cmat = outmap[slot]
        high = state[g].astype(BF16)
        low = (state[g] - high.astype(F32)).astype(BF16)
        carried[slot] = dot(
            jnp.concatenate([high, low], axis=1), jnp.concatenate([cmat, cmat], axis=0)
        )
        for h in range(HEADS):
            span = slice(h * HEAD_DIM, (h + 1) * HEAD_DIM)
            wgt[span, :] = (act[slot, span, :].astype(F32) * until[h : h + 1, :]).astype(BF16)
        update = dot(wgt[...], into[slot])
        for h in range(HEADS):
            span = slice(h * HEAD_DIM, (h + 1) * HEAD_DIM)
            state[g, span, :] = state[g, span, :] * fade[h : h + 1, :] + update[span, :]
        return 0

    def mix(u, _):
        c = u // GROUPS
        g = lax.rem(u, GROUPS)
        slot = lax.rem(u, HELD)
        lay_out_gates(c, g)
        scores = dot(into[slot], outmap[slot])
        columns = within[slot]
        for pair in range(HEADS // 2):
            owns = []
            reaches = []
            for h in (2 * pair, 2 * pair + 1):
                span = slice(h * HEAD_DIM, (h + 1) * HEAD_DIM)
                gaps = small[slot, 0, h : h + 1, :] - columns[:, h : h + 1]
                weights = (scores * jnp.exp(jnp.where(causal, gaps, -jnp.inf))).astype(BF16)
                x = act[slot, span, :]
                mixed = (
                    dot(x, weights)
                    + params[2, g, h : h + 1, :] * x.astype(F32)
                    + carried[slot, span, :] * small[slot, 1, h : h + 1, :]
                )
                gate = silu(gates[span, :])
                owns.append(mixed * gate)
                reaches.append(gate * small[slot, 2, h : h + 1, :])
            span = slice(pair * 2 * HEAD_DIM, (pair + 1) * 2 * HEAD_DIM)
            turned_own[u, :, span] = jnp.transpose(jnp.concatenate(owns, axis=0))
            turned_gate[u, :, span] = jnp.transpose(jnp.concatenate(reaches, axis=0))
        return 0

    def unit(u, _):
        advance(u, 0)
        mix(u, 0)
        return 0

    units = CHUNKS * GROUPS
    lax.fori_loop(0, units - HELD, unit, 0)
    lax.fori_loop(units - HELD, units, advance, 0)

    low_sub = lax.broadcasted_iota(jnp.int32, (16, CHUNK), 0)
    for g in range(GROUPS):
        for h in range(HEADS):
            first = (g * HEADS + h) * MESSAGE
            own[first : first + HEAD_DIM, :] = state[
                g, h * HEAD_DIM : (h + 1) * HEAD_DIM, :
            ].astype(BF16)
            fade = jnp.broadcast_to(jnp.exp(lead[g, h : h + 1, :]), (16, CHUNK))
            high = fade.astype(BF16).astype(F32)
            middle = (fade - high).astype(BF16).astype(F32)
            parts = jnp.where(
                low_sub == 0,
                high,
                jnp.where(
                    low_sub == 1, middle, jnp.where(low_sub == 2, fade - high - middle, 0.0)
                ),
            )
            own[first + HEAD_DIM : first + MESSAGE, :] = parts.astype(BF16)

    def heads_of(ref, device, height):
        size = per_device * height
        return ref.at[pl.ds(pl.multiple_of(device * size, size), size)]

    def wait_all(ref, sem, height):
        peers = ref.at[pl.ds(0, (n - 1) * per_device * height)]
        pltpu.make_async_copy(peers, peers, sem).wait()

    def send_heads(source, target, height, send_sem, recv_sem):
        def send(i, _):
            device = peer(i, 0)
            pltpu.make_async_remote_copy(
                src_ref=heads_of(source, device, height),
                dst_ref=heads_of(target, me, height),
                send_sem=send_sem,
                recv_sem=recv_sem,
                device_id={"seq": device},
                device_id_type=MESH,
            ).start()
            return 0

        lax.fori_loop(0, n - 1, send, 0)
        heads_of(target, me, height)[...] = heads_of(source, me, height)[...]

    send_heads(own, gathered, MESSAGE, scan_send, scan_recv)
    lax.fori_loop(units - HELD, units, mix, 0)
    wait_all(gathered, scan_recv, MESSAGE)

    def horner(device, reached):
        heads_of(prefix, device, HEAD_DIM)[...] = reached.astype(BF16)
        message = heads_of(gathered, device, MESSAGE)[...].astype(F32)
        terms = []
        for h in range(per_device):
            first = h * MESSAGE
            fade = jnp.sum(message[first + HEAD_DIM : first + MESSAGE, :], axis=0, keepdims=True)
            terms.append(
                reached[h * HEAD_DIM : (h + 1) * HEAD_DIM, :] * fade
                + message[first : first + HEAD_DIM, :]
            )
        return terms[0] if per_device == 1 else jnp.concatenate(terms, axis=0)

    lax.fori_loop(0, n, horner, jnp.zeros((per_device * HEAD_DIM, STATE_WIDTH), F32))
    send_heads(prefix, incoming, HEAD_DIM, back_send, back_recv)
    wait_all(incoming, back_recv, HEAD_DIM)

    def finish(u, _):
        c = u // GROUPS
        g = lax.rem(u, GROUPS)
        arrived = dot_nt(
            outrows[u], incoming[pl.ds(pl.multiple_of(g * SPAN, SPAN), SPAN), :]
        )
        for i in range(CHUNK // 16):
            span = slice(i * 16, (i + 1) * 16)
            gated = turned_own[u, span, :] + arrived[span, :] * turned_gate[u, span, :]
            squares = jnp.sum(gated * gated, axis=1, keepdims=True)
            scale = lax.rsqrt(squares * (1.0 / SPAN) + EPSILON)
            staged[u, span, :] = (gated * scale * gain_ref[g]).astype(BF16)
        pltpu.make_async_copy(
            staged.at[u],
            out_ref.at[
                pl.ds(pl.multiple_of(c * CHUNK, CHUNK), CHUNK),
                pl.ds(pl.multiple_of(g * SPAN, SPAN), SPAN),
            ],
            out_sem,
        ).start()
        return 0

    lax.fori_loop(0, units, finish, 0)

    def drain(c, _):
        peers = recv.at[c, pl.ds(0, n - 1)]
        pltpu.make_async_copy(peers, peers, chunk_send.at[c]).wait()
        return 0

    lax.fori_loop(0, CHUNKS, drain, 0)
    wait_all(own, scan_send, MESSAGE)
    wait_all(prefix, back_send, HEAD_DIM)
    pltpu.make_async_copy(staged, staged, out_sem).wait()


def per_device(projected, conv_weight, dt_bias, a_log, d_skip, norm_gain):
    n = lax.axis_size("seq")
    slab = COLS * GROUPS // n
    tokens = CHUNK * CHUNKS
    units = GROUPS * CHUNKS
    heads = GROUPS * HEADS
    hbm = pl.BlockSpec(memory_space=pltpu.HBM)
    anywhere = pl.BlockSpec(memory_space=pl.ANY)
    dma = pltpu.SemaphoreType.DMA
    return pl.pallas_call(
        functools.partial(kernel, n),
        out_shape=jax.ShapeDtypeStruct((tokens, GROUPS * SPAN), BF16),
        in_specs=[hbm] * 6,
        out_specs=anywhere,
        scratch_shapes=[
            pltpu.VMEM((4, GROUPS, CONV), F32),
            pltpu.VMEM((1, heads), F32),
            pltpu.VMEM((1, heads), F32),
            pltpu.VMEM((1, heads), F32),
            pltpu.VMEM((GROUPS, 1, SPAN), F32),
            pltpu.VMEM((CHUNKS, n, slab, CHUNK), BF16),
            pltpu.VMEM((COLS, CHUNK), F32),
            pltpu.VMEM((-(-SPAN // slab) * slab, CHUNK), F32),
            pltpu.VMEM((GROUPS, 4, CONV, CHUNK), F32),
            pltpu.VMEM((3, GROUPS, HEADS, CHUNK), F32),
            pltpu.VMEM((GROUPS, CONV, CHUNK), F32),
            pltpu.VMEM((HELD, SPAN, CHUNK), BF16),
            pltpu.VMEM((SPAN, CHUNK), BF16),
            pltpu.VMEM((GROUPS, SPAN, STATE_WIDTH), F32),
            pltpu.VMEM((HELD, SPAN, CHUNK), F32),
            pltpu.VMEM((HELD, CHUNK, CHUNK), F32),
            pltpu.VMEM((HELD, CHUNK, STATE_WIDTH), BF16),
            pltpu.VMEM((HELD, STATE_WIDTH, CHUNK), BF16),
            pltpu.VMEM((units, CHUNK, STATE_WIDTH), BF16),
            pltpu.VMEM((HELD, 3, HEADS, CHUNK), F32),
            pltpu.VMEM((GROUPS, HEADS, CHUNK), F32),
            pltpu.VMEM((units, CHUNK, SPAN), F32),
            pltpu.VMEM((units, CHUNK, SPAN), F32),
            pltpu.VMEM((GROUPS, 8, CONV), F32),
            pltpu.VMEM((GROUPS, 8, CONV), F32),
            pltpu.VMEM((heads * MESSAGE, STATE_WIDTH), BF16),
            pltpu.VMEM((heads * MESSAGE, STATE_WIDTH), BF16),
            pltpu.VMEM((heads * HEAD_DIM, STATE_WIDTH), BF16),
            pltpu.VMEM((heads * HEAD_DIM, STATE_WIDTH), BF16),
            pltpu.VMEM((units, CHUNK, SPAN), BF16),
            dma((CHUNKS,)), dma((CHUNKS,)), dma((CHUNKS,)), dma, dma,
            dma, dma, dma, dma, dma, dma((5,)),
        ],
        compiler_params=pltpu.CompilerParams(
            collective_id=0, has_side_effects=True, vmem_limit_bytes=48 * 2**20
        ),
    )(
        projected, conv_weight,
        dt_bias.reshape(1, heads), a_log.reshape(1, heads), d_skip.reshape(1, heads),
        norm_gain.reshape(GROUPS, 1, SPAN),
    )


def solution(mesh):
    in_specs = (P(("tp", "seq"), None), P(None, "tp", None), P("tp"), P("tp"), P("tp"), P("tp"))
    return jax.shard_map(
        per_device, mesh=mesh, in_specs=in_specs, out_specs=P("seq", "tp"), check_vma=False
    )
```

time: 179 us -> 154 us (0.86)
  Pallas kernels: 171 us -> 149 us
  local copies, waits for them, and re-layouts: 7.69 us -> 5.45 us
    pallas_call x1, Pallas kernels: 171 us -> 149 us  [per_device(): pl.pallas_call(functools.partial(kernel, n), out_shape=jax.ShapeDtypeStru...]
    another operation x3 -> x0, local copies, waits for them, and re-layouts: 2.2 us -> none  [per_device(): jnp.stack([dt_bias, a_log, d_skip]).reshape(3, GROUPS, HEADS, 1)]
    unnamed x1 -> x11, local copies, waits for them, and re-layouts: 4.79 us -> 5.45 us
where the time goes in v2:
time: 154 us
  Pallas kernels  149 us (97%)
  local copies, waits for them, and re-layouts  5.45 us (4%)
    pallas_call x1, Pallas kernels, per_device(): pl.pallas_call(functools.partial(kernel, n), out_shape=jax.ShapeDtypeStru...  149 us
    unnamed x11, local copies, waits for them, and re-layouts  5.45 us

profile of v2, /device:TPU:1, one launch (start us, length us, event | category | flops | bytes accessed | tf_op | source)
XLA Modules:
  0.0 154.2 jit_solution(14534973450999798242)
XLA Ops:
  0.0 0.0 copy-start
  0.0 0.8 copy-done
  0.8 0.0 copy-start.1
  0.8 0.7 copy-done.1
  1.5 0.0 copy-start.2
  1.5 0.7 copy-done.2
  2.1 0.0 copy-start.3
  2.1 0.7 copy-done.3
  2.8 0.0 copy-start.4
  2.8 0.7 copy-done.4
  3.4 148.8 %shard_map.64 = bf16[1024,2048]{1,0:T(8,128)(2,1)S(1)} custom-call(bf16[145,32768]{1,0:T(8,128)(2,1)} %x_ref.1, f32[4,2,1280]{2,1,0:T(2,128)S(1)} %copy-done, f32[1,32]{1,0:T(1,128)S(1)} %bitcast.5, f32[1,32]{1,0:T(1,128)S(1)} %bitcast.6, f32[1,32]{1,0:T(1,128)S(1)} %bitcast.7, f32[2,1,1024]{2,1,0:T(1,128)S(1)} %bitcast.4), custom_call_target="tpu_custom_call" | custom-call | tf_op jit(solution)/shard_map/pallas_call | solution.py:397
  152.2 2.0 %copy.8 = bf16[1024,2048]{1,0:T(8,128)(2,1)} copy(bf16[1024,2048]{1,0:T(8,128)(2,1)S(1)} %shard_map.64) | data formatting | bytes 8388608
Async XLA Ops:
  0.0 0.8 copy-start
  0.8 0.7 copy-start.1
  1.5 0.7 copy-start.2
  2.1 0.7 copy-start.3
  2.8 0.7 copy-start.4

commit v3 on v2

--- a/solution.py
+++ b/solution.py
@@ -19,7 +19,8 @@
 COLS = SPAN + CONV + HEADS
 EPSILON = 1e-05
 AHEAD = 3
-HELD = 4
+CONV_ROWS = 4 * GROUPS * CONV // CHUNK
+HELD = 2
 MESSAGE = HEAD_DIM + 16
 
 F32 = jnp.float32
@@ -39,32 +40,32 @@
 
 
 def kernel(
-    n, x_ref, conv_hbm, bias_hbm, rate_hbm, skip_hbm, gain_hbm, out_ref,
-    conv_ref, bias_ref, rate_ref, skip_ref, gain_ref, recv, rows, gates, taps, params, prev, act, wgt, state, carried, within, into,
+    n, x_ref, pack_hbm, out_ref,
+    pack_ref, recv, rows, gates, taps, params, prev, act, wgt, state, carried, within, into,
     outmap, outrows, small, lead, turned_gate, turned_own,
-    halo_out, halo_in, own, gathered, prefix, incoming, staged,
-    chunk_send, chunk_recv, chunk_own, halo_send, halo_recv,
+    tails, spare, extra_out, extra_in, extra, own, gathered, prefix, incoming, staged,
+    chunk_send, chunk_recv, chunk_own, extra_send, extra_recv, tail_sem, spare_sem,
     scan_send, scan_recv, back_send, back_recv, out_sem, small_sem,
 ):
     me = lax.axis_index("seq")
     slab = COLS * GROUPS // n
+    body = slab - 1
     per_group = n // GROUPS
     per_device = GROUPS * HEADS // n
 
-    loads = [
-        pltpu.make_async_copy(source, target, small_sem.at[k])
-        for k, (source, target) in enumerate(
-            (
-                (conv_hbm, conv_ref),
-                (bias_hbm, bias_ref),
-                (rate_hbm, rate_ref),
-                (skip_hbm, skip_ref),
-                (gain_hbm, gain_ref),
-            )
-        )
-    ]
-    for load in loads:
-        load.start()
+    load = pltpu.make_async_copy(pack_hbm, pack_ref, small_sem)
+    load.start()
+    spare_load = pltpu.make_async_copy(x_ref.at[pl.ds(body, 1), :], spare, spare_sem)
+    spare_load.start()
+
+    def load_tail(device, _):
+        first = pl.multiple_of((device + 1) * CHUNK * CHUNKS - CHUNK, CHUNK)
+        pltpu.make_async_copy(
+            x_ref.at[:, pl.ds(first, CHUNK)], tails.at[device], tail_sem
+        ).start()
+        return 0
+
+    lax.fori_loop(0, n, load_tail, 0)
 
     barrier = pltpu.get_barrier_semaphore()
 
@@ -88,10 +89,9 @@
 
     def piece(device, c):
         first = pl.multiple_of(device * (CHUNK * CHUNKS) + c * CHUNK, CHUNK)
-        return x_ref.at[:, pl.ds(first, CHUNK)]
-
-    def send_chunk(turn, _):
-        c = lax.rem(turn + CHUNKS - 1, CHUNKS)
+        return x_ref.at[pl.ds(0, body), pl.ds(first, CHUNK)]
+
+    def send_chunk(c, _):
 
         def send(i, _):
             device = peer(i, c * 5)
@@ -109,7 +109,47 @@
         pltpu.make_async_copy(piece(me, c), recv.at[c, me], chunk_own.at[c]).start()
         return 0
 
-    lax.fori_loop(0, AHEAD, send_chunk, 0)
+    send_chunk(0, 0)
+    pltpu.make_async_copy(tails, tails, tail_sem).wait()
+    spare_load.wait()
+
+    def make_extra(device, _):
+        before = lax.rem(device + n - 1, n)
+        has_past = jnp.where(device > 0, 1.0, 0.0).astype(F32)
+        tail = tails[before].astype(F32) * has_past
+        first = jnp.transpose(tail[:CHUNK, :])
+        second = jnp.transpose(
+            jnp.concatenate([tail[CHUNK:, :], jnp.zeros((2 * CHUNK - slab, CHUNK), F32)], axis=0)
+        )
+        held = [
+            spare[
+                :, pl.ds(pl.multiple_of(device * (CHUNK * CHUNKS) + c * CHUNK, CHUNK), CHUNK)
+            ].astype(F32)
+            for c in range(CHUNKS)
+        ]
+        extra_out[device] = jnp.concatenate(
+            held + [first[CHUNK - 3 :, :], second[CHUNK - 3 :, :], jnp.zeros((2, CHUNK), F32)],
+            axis=0,
+        ).astype(BF16)
+        return 0
+
+    lax.fori_loop(0, n, make_extra, 0)
+
+    def send_extra(i, _):
+        device = peer(i, 0)
+        pltpu.make_async_remote_copy(
+            src_ref=extra_out.at[device],
+            dst_ref=extra_in.at[me],
+            send_sem=extra_send,
+            recv_sem=extra_recv,
+            device_id={"seq": device},
+            device_id_type=MESH,
+        ).start()
+        return 0
+
+    lax.fori_loop(0, n - 1, send_extra, 0)
+    extra_in[me] = extra_out[me]
+    lax.fori_loop(1, AHEAD + 1, send_chunk, 0)
 
     def wait_chunk(c):
         peers = recv.at[c, pl.ds(0, n - 1)]
@@ -120,12 +160,14 @@
     lane = lax.broadcasted_iota(jnp.int32, (CHUNK, CHUNK), 1)
     causal = sub <= lane
 
-    for load in loads:
-        load.wait()
+    load.wait()
 
     def taps_of(g, i):
         four = jnp.concatenate(
-            [conv_ref[k, g : g + 1, i * CHUNK : (i + 1) * CHUNK] for k in range(4)]
+            [
+                pack_ref[pl.ds((k * GROUPS + g) * (CONV // CHUNK) + i, 1), :]
+                for k in range(4)
+            ]
             + [jnp.zeros((CHUNK - 4, CHUNK), F32)],
             axis=0,
         )
@@ -139,8 +181,7 @@
         for i in range(CONV // CHUNK):
             taps_of(g, i)
     rows[0:CHUNK, :] = jnp.zeros((CHUNK, CHUNK), F32)
-    for k, ref in enumerate((bias_ref, rate_ref, skip_ref)):
-        rows[k : k + 1, 0 : GROUPS * HEADS] = ref[...]
+    rows[0:8, :] = pack_ref[CONV_ROWS : CONV_ROWS + 8, :]
     turned = jnp.transpose(rows[0:CHUNK, :])
     for k in range(3):
         for g in range(GROUPS):
@@ -150,48 +191,49 @@
     lead[...] = jnp.zeros_like(lead)
     state[...] = jnp.zeros_like(state)
 
+    def lay_rows(target, c, g, first, end):
+        for k in range(first, end):
+            target[k * slab : k * slab + body, :] = recv[c, g * per_group + k].astype(F32)
+            target[k * slab + body : (k + 1) * slab, :] = extra[
+                g * per_group + k, pl.ds(c, 1), :
+            ]
+
     def lay_out(c, g):
+        lay_rows(rows, c, g, SPAN // slab, per_group)
+
+    def lay_out_gates(c, g):
+        lay_rows(gates, c, g, 0, -(-SPAN // slab))
+
+    extras = extra_in.at[pl.ds(0, n - 1)]
+    pltpu.make_async_copy(extras, extras, extra_recv).wait()
+
+    def read_extra(device, _):
+        extra[device] = extra_in[device].astype(F32)[:CHUNKS, :]
+        return 0
+
+    lax.fori_loop(0, n, read_extra, 0)
+    blank = jnp.zeros((CHUNK - 3, CHUNK), F32)
+
+    def read_past(g, _):
         for k in range(SPAN // slab, per_group):
-            rows[k * slab : (k + 1) * slab, :] = recv[c, g * per_group + k].astype(F32)
-
-    def lay_out_gates(c, g):
-        for k in range(-(-SPAN // slab)):
-            gates[k * slab : (k + 1) * slab, :] = recv[c, g * per_group + k].astype(F32)
-
-    wait_chunk(CHUNKS - 1)
-    send_chunk(AHEAD, 0)
-
-    def make_halo(g, _):
-        lay_out(CHUNKS - 1, g)
+            message = extra_in[g * per_group + k].astype(F32)
+            first = jnp.transpose(jnp.concatenate([blank, message[8:11, :]], axis=0))
+            second = jnp.transpose(jnp.concatenate([blank, message[11:14, :]], axis=0))
+            rows[k * slab : k * slab + CHUNK, :] = first
+            rows[k * slab + CHUNK : (k + 1) * slab, :] = second[: slab - CHUNK, :]
         for i in range(CONV // CHUNK):
-            tile = rows[SPAN + i * CHUNK : SPAN + (i + 1) * CHUNK, :]
-            halo_out[g, :, i * CHUNK : (i + 1) * CHUNK] = jnp.transpose(tile)[CHUNK - 8 :, :]
-        return 0
-
-    lax.fori_loop(0, GROUPS, make_halo, 0)
-    halo_copy = pltpu.make_async_remote_copy(
-        src_ref=halo_out,
-        dst_ref=halo_in,
-        send_sem=halo_send,
-        recv_sem=halo_recv,
-        device_id={"seq": lax.rem(me + 1, n)},
-        device_id_type=MESH,
-    )
-    halo_copy.start()
-    halo_copy.wait()
-    has_past = jnp.where(me > 0, 1.0, 0.0).astype(F32)
-    for g in range(GROUPS):
-        for i in range(CONV // CHUNK):
-            tail = halo_in[g, :, i * CHUNK : (i + 1) * CHUNK] * has_past
-            tile = jnp.concatenate([jnp.zeros((CHUNK - 8, CHUNK), F32), tail], axis=0)
-            prev[g, i * CHUNK : (i + 1) * CHUNK, :] = jnp.transpose(tile)
+            span = slice(i * CHUNK, (i + 1) * CHUNK)
+            prev[g, span, :] = rows[SPAN + i * CHUNK : SPAN + (i + 1) * CHUNK, :]
+        return 0
+
+    lax.fori_loop(0, GROUPS, read_past, 0)
 
     def advance(u, _):
         c = u // GROUPS
         g = lax.rem(u, GROUPS)
         slot = lax.rem(u, HELD)
 
-        @pl.when(jnp.logical_and(g == 0, c < CHUNKS - 1))
+        @pl.when(g == 0)
         def _():
             wait_chunk(c)
 
@@ -353,6 +395,13 @@
     def finish(u, _):
         c = u // GROUPS
         g = lax.rem(u, GROUPS)
+        gain = jnp.concatenate(
+            [
+                pack_ref[pl.ds(CONV_ROWS + 8 + g * (SPAN // CHUNK) + i, 1), :]
+                for i in range(SPAN // CHUNK)
+            ],
+            axis=1,
+        )
         arrived = dot_nt(
             outrows[u], incoming[pl.ds(pl.multiple_of(g * SPAN, SPAN), SPAN), :]
         )
@@ -361,7 +410,7 @@
             gated = turned_own[u, span, :] + arrived[span, :] * turned_gate[u, span, :]
             squares = jnp.sum(gated * gated, axis=1, keepdims=True)
             scale = lax.rsqrt(squares * (1.0 / SPAN) + EPSILON)
-            staged[u, span, :] = (gated * scale * gain_ref[g]).astype(BF16)
+            staged[u, span, :] = (gated * scale * gain).astype(BF16)
         pltpu.make_async_copy(
             staged.at[u],
             out_ref.at[
@@ -380,6 +429,7 @@
         return 0
 
     lax.fori_loop(0, CHUNKS, drain, 0)
+    pltpu.make_async_copy(extras, extras, extra_send).wait()
     wait_all(own, scan_send, MESSAGE)
     wait_all(prefix, back_send, HEAD_DIM)
     pltpu.make_async_copy(staged, staged, out_sem).wait()
@@ -391,21 +441,26 @@
     tokens = CHUNK * CHUNKS
     units = GROUPS * CHUNKS
     heads = GROUPS * HEADS
+    scalars = jnp.stack([dt_bias, a_log, d_skip])
+    packed = jnp.concatenate(
+        [
+            conv_weight.reshape(-1, CHUNK),
+            jnp.pad(scalars, ((0, 5), (0, CHUNK - heads))),
+            norm_gain.reshape(-1, CHUNK),
+        ],
+        axis=0,
+    )
     hbm = pl.BlockSpec(memory_space=pltpu.HBM)
     anywhere = pl.BlockSpec(memory_space=pl.ANY)
     dma = pltpu.SemaphoreType.DMA
     return pl.pallas_call(
         functools.partial(kernel, n),
         out_shape=jax.ShapeDtypeStruct((tokens, GROUPS * SPAN), BF16),
-        in_specs=[hbm] * 6,
+        in_specs=[hbm] * 2,
         out_specs=anywhere,
         scratch_shapes=[
-            pltpu.VMEM((4, GROUPS, CONV), F32),
-            pltpu.VMEM((1, heads), F32),
-            pltpu.VMEM((1, heads), F32),
-            pltpu.VMEM((1, heads), F32),
-            pltpu.VMEM((GROUPS, 1, SPAN), F32),
-            pltpu.VMEM((CHUNKS, n, slab, CHUNK), BF16),
+            pltpu.VMEM(packed.shape, F32),
+            pltpu.VMEM((CHUNKS, n, slab - 1, CHUNK), BF16),
             pltpu.VMEM((COLS, CHUNK), F32),
             pltpu.VMEM((-(-SPAN // slab) * slab, CHUNK), F32),
             pltpu.VMEM((GROUPS, 4, CONV, CHUNK), F32),
@@ -423,23 +478,24 @@
             pltpu.VMEM((GROUPS, HEADS, CHUNK), F32),
             pltpu.VMEM((units, CHUNK, SPAN), F32),
             pltpu.VMEM((units, CHUNK, SPAN), F32),
-            pltpu.VMEM((GROUPS, 8, CONV), F32),
-            pltpu.VMEM((GROUPS, 8, CONV), F32),
+            pltpu.VMEM((n, slab, CHUNK), BF16),
+            pltpu.VMEM((1, n * tokens), BF16),
+            pltpu.VMEM((n, 16, CHUNK), BF16),
+            pltpu.VMEM((n, 16, CHUNK), BF16),
+            pltpu.VMEM((n, CHUNKS, CHUNK), F32),
             pltpu.VMEM((heads * MESSAGE, STATE_WIDTH), BF16),
             pltpu.VMEM((heads * MESSAGE, STATE_WIDTH), BF16),
             pltpu.VMEM((heads * HEAD_DIM, STATE_WIDTH), BF16),
             pltpu.VMEM((heads * HEAD_DIM, STATE_WIDTH), BF16),
             pltpu.VMEM((units, CHUNK, SPAN), BF16),
-            dma((CHUNKS,)), dma((CHUNKS,)), dma((CHUNKS,)), dma, dma,
-            dma, dma, dma, dma, dma, dma((5,)),
+            dma((CHUNKS,)), dma((CHUNKS,)), dma((CHUNKS,)), dma, dma, dma, dma,
+            dma, dma, dma, dma, dma, dma,
         ],
         compiler_params=pltpu.CompilerParams(
             collective_id=0, has_side_effects=True, vmem_limit_bytes=48 * 2**20
         ),
     )(
-        projected, conv_weight,
-        dt_bias.reshape(1, heads), a_log.reshape(1, heads), d_skip.reshape(1, heads),
-        norm_gain.reshape(GROUPS, 1, SPAN),
+        projected, packed
     )
 
 

time: 154 us -> 147 us (0.955)
  Pallas kernels: 149 us -> 143 us
  local copies, waits for them, and re-layouts: 5.45 us -> 2.83 us
    pallas_call x1, Pallas kernels: 149 us -> 143 us  [per_device(): pl.pallas_call(functools.partial(kernel, n), out_shape=jax.ShapeDtypeStru...]
    unnamed x11 -> x1, local copies, waits for them, and re-layouts: 5.45 us -> 2.02 us
where the time goes in v3:
time: 147 us
  Pallas kernels  143 us (97%)
  local copies, waits for them, and re-layouts  2.83 us (2%)
    pallas_call x1, Pallas kernels, per_device(): pl.pallas_call(functools.partial(kernel, n), out_shape=jax.ShapeDtypeStru...  143 us

profile of v3, /device:TPU:1, one launch (start us, length us, event | category | flops | bytes accessed | tf_op | source)
XLA Modules:
  0.0 147.0 jit_solution(16888938407869047776)
XLA Ops:
  0.0 0.7 select_maximum_fusion
  0.7 0.8 reshape.6
  1.5 0.7 pad_maximum_fusion.pack_hbm
  2.2 142.8 %shard_map.64 = bf16[1024,2048]{1,0:T(8,128)(2,1)S(1)} custom-call(bf16[145,32768]{1,0:T(8,128)(2,1)} %x_ref.1, f32[104,128]{1,0:T(8,128)S(1)} %pad_maximum_fusion.pack_hbm), custom_call_target="tpu_custom_call" | custom-call | tf_op jit(solution)/shard_map/pallas_call | solution.py:456
  145.0 2.0 %copy.8 = bf16[1024,2048]{1,0:T(8,128)(2,1)} copy(bf16[1024,2048]{1,0:T(8,128)(2,1)S(1)} %shard_map.64) | data formatting | bytes 8388608

commit v4 on v3

--- a/solution.py
+++ b/solution.py
@@ -35,15 +35,11 @@
     return jnp.dot(a, b, preferred_element_type=F32, precision=precision)
 
 
-def dot_nt(a, b):
-    return lax.dot_general(a, b, (((1,), (1,)), ((), ())), preferred_element_type=F32)
-
-
 def kernel(
     n, x_ref, pack_hbm, out_ref,
     pack_ref, recv, rows, gates, taps, params, prev, act, wgt, state, carried, within, into,
     outmap, outrows, small, lead, turned_gate, turned_own,
-    tails, spare, extra_out, extra_in, extra, own, gathered, prefix, incoming, staged,
+    tails, spare, extra_out, extra_in, extra, own, gathered, prefix, incoming, turned_in, staged,
     chunk_send, chunk_recv, chunk_own, extra_send, extra_recv, tail_sem, spare_sem,
     scan_send, scan_recv, back_send, back_recv, out_sem, small_sem,
 ):
@@ -51,7 +47,6 @@
     slab = COLS * GROUPS // n
     body = slab - 1
     per_group = n // GROUPS
-    per_device = GROUPS * HEADS // n
 
     load = pltpu.make_async_copy(pack_hbm, pack_ref, small_sem)
     load.start()
@@ -326,12 +321,21 @@
 
     units = CHUNKS * GROUPS
     lax.fori_loop(0, units - HELD, unit, 0)
-    lax.fori_loop(units - HELD, units, advance, 0)
 
     low_sub = lax.broadcasted_iota(jnp.int32, (16, CHUNK), 0)
+
+    def head_at(ref, position, height):
+        return ref.at[pl.ds(pl.multiple_of(position * height, height), height)]
+
+    def wait_messages(ref, count, height, sem):
+        messages = ref.at[pl.ds(0, count * height)]
+        pltpu.make_async_copy(messages, messages, sem).wait()
+
+    mine = lax.rem(me, GROUPS)
     for g in range(GROUPS):
+        advance(units - HELD + g, 0)
         for h in range(HEADS):
-            first = (g * HEADS + h) * MESSAGE
+            first = (h * GROUPS + g) * MESSAGE
             own[first : first + HEAD_DIM, :] = state[
                 g, h * HEAD_DIM : (h + 1) * HEAD_DIM, :
             ].astype(BF16)
@@ -347,81 +351,102 @@
             )
             own[first + HEAD_DIM : first + MESSAGE, :] = parts.astype(BF16)
 
-    def heads_of(ref, device, height):
-        size = per_device * height
-        return ref.at[pl.ds(pl.multiple_of(device * size, size), size)]
-
-    def wait_all(ref, sem, height):
-        peers = ref.at[pl.ds(0, (n - 1) * per_device * height)]
-        pltpu.make_async_copy(peers, peers, sem).wait()
-
-    def send_heads(source, target, height, send_sem, recv_sem):
-        def send(i, _):
-            device = peer(i, 0)
-            pltpu.make_async_remote_copy(
-                src_ref=heads_of(source, device, height),
-                dst_ref=heads_of(target, me, height),
-                send_sem=send_sem,
-                recv_sem=recv_sem,
-                device_id={"seq": device},
-                device_id_type=MESH,
+        def send_state(i, _):
+            move = lax.rem(i * 5 + 6, HEADS)
+            y = lax.rem(me // 8 + move // 4, 4)
+            x = lax.rem(me // 2 + move, 4)
+            device = y * 8 + x * 2 + g
+
+            @pl.when(device != me)
+            def _():
+                pltpu.make_async_remote_copy(
+                    src_ref=head_at(own, device, MESSAGE),
+                    dst_ref=head_at(gathered, me, MESSAGE),
+                    send_sem=scan_send,
+                    recv_sem=scan_recv,
+                    device_id={"seq": device},
+                    device_id_type=MESH,
+                ).start()
+
+            return 0
+
+        lax.fori_loop(0, HEADS, send_state, 0)
+    head_at(gathered, me, MESSAGE)[...] = head_at(own, me, MESSAGE)[...]
+
+    @pl.when(mine == 1)
+    def _():
+        lax.fori_loop(units - HELD, units, mix, 0)
+
+    wait_messages(gathered, n - 1, MESSAGE, scan_recv)
+
+    def horner(device, reached):
+        head_at(prefix, device, HEAD_DIM)[...] = reached.astype(BF16)
+        message = head_at(gathered, device, MESSAGE)[...].astype(F32)
+        fade = jnp.sum(message[HEAD_DIM:, :], axis=0, keepdims=True)
+        return reached * fade + message[:HEAD_DIM, :]
+
+    lax.fori_loop(0, n, horner, jnp.zeros((HEAD_DIM, STATE_WIDTH), F32))
+    slot = mine * HEADS + me // GROUPS
+
+    def send_back(i, _):
+        device = peer(i, 0)
+        pltpu.make_async_remote_copy(
+            src_ref=head_at(prefix, device, HEAD_DIM),
+            dst_ref=head_at(incoming, slot, HEAD_DIM),
+            send_sem=back_send,
+            recv_sem=back_recv.at[mine],
+            device_id={"seq": device},
+            device_id_type=MESH,
+        ).start()
+        return 0
+
+    lax.fori_loop(0, n - 1, send_back, 0)
+    head_at(incoming, slot, HEAD_DIM)[...] = head_at(prefix, me, HEAD_DIM)[...]
+
+    @pl.when(mine == 0)
+    def _():
+        lax.fori_loop(units - HELD, units, mix, 0)
+
+    for g in range(GROUPS):
+
+        @pl.when(mine == g)
+        def _():
+            wait_messages(incoming, HEADS - 1, HEAD_DIM, back_recv.at[g])
+
+        @pl.when(mine != g)
+        def _():
+            wait_messages(incoming, HEADS, HEAD_DIM, back_recv.at[g])
+
+        for i in range(SPAN // CHUNK):
+            block = incoming[g * SPAN + i * CHUNK : g * SPAN + (i + 1) * CHUNK, :]
+            turned_in[:, i * CHUNK : (i + 1) * CHUNK] = jnp.transpose(block.astype(F32)).astype(
+                BF16
+            )
+        first = CONV_ROWS + 8 + g * (SPAN // CHUNK)
+        gain = jnp.concatenate(
+            [pack_ref[first + i : first + i + 1, :] for i in range(SPAN // CHUNK)], axis=1
+        )
+
+        def finish(c, _):
+            u = c * GROUPS + g
+            arrived = dot(outrows[u], turned_in[...])
+            for i in range(CHUNK // 16):
+                span = slice(i * 16, (i + 1) * 16)
+                gated = turned_own[u, span, :] + arrived[span, :] * turned_gate[u, span, :]
+                squares = jnp.sum(gated * gated, axis=1, keepdims=True)
+                scale = lax.rsqrt(squares * (1.0 / SPAN) + EPSILON)
+                staged[u, span, :] = (gated * scale * gain).astype(BF16)
+            pltpu.make_async_copy(
+                staged.at[u],
+                out_ref.at[
+                    pl.ds(pl.multiple_of(c * CHUNK, CHUNK), CHUNK),
+                    pl.ds(g * SPAN, SPAN),
+                ],
+                out_sem,
             ).start()
             return 0
 
-        lax.fori_loop(0, n - 1, send, 0)
-        heads_of(target, me, height)[...] = heads_of(source, me, height)[...]
-
-    send_heads(own, gathered, MESSAGE, scan_send, scan_recv)
-    lax.fori_loop(units - HELD, units, mix, 0)
-    wait_all(gathered, scan_recv, MESSAGE)
-
-    def horner(device, reached):
-        heads_of(prefix, device, HEAD_DIM)[...] = reached.astype(BF16)
-        message = heads_of(gathered, device, MESSAGE)[...].astype(F32)
-        terms = []
-        for h in range(per_device):
-            first = h * MESSAGE
-            fade = jnp.sum(message[first + HEAD_DIM : first + MESSAGE, :], axis=0, keepdims=True)
-            terms.append(
-                reached[h * HEAD_DIM : (h + 1) * HEAD_DIM, :] * fade
-                + message[first : first + HEAD_DIM, :]
-            )
-        return terms[0] if per_device == 1 else jnp.concatenate(terms, axis=0)
-
-    lax.fori_loop(0, n, horner, jnp.zeros((per_device * HEAD_DIM, STATE_WIDTH), F32))
-    send_heads(prefix, incoming, HEAD_DIM, back_send, back_recv)
-    wait_all(incoming, back_recv, HEAD_DIM)
-
-    def finish(u, _):
-        c = u // GROUPS
-        g = lax.rem(u, GROUPS)
-        gain = jnp.concatenate(
-            [
-                pack_ref[pl.ds(CONV_ROWS + 8 + g * (SPAN // CHUNK) + i, 1), :]
-                for i in range(SPAN // CHUNK)
-            ],
-            axis=1,
-        )
-        arrived = dot_nt(
-            outrows[u], incoming[pl.ds(pl.multiple_of(g * SPAN, SPAN), SPAN), :]
-        )
-        for i in range(CHUNK // 16):
-            span = slice(i * 16, (i + 1) * 16)
-            gated = turned_own[u, span, :] + arrived[span, :] * turned_gate[u, span, :]
-            squares = jnp.sum(gated * gated, axis=1, keepdims=True)
-            scale = lax.rsqrt(squares * (1.0 / SPAN) + EPSILON)
-            staged[u, span, :] = (gated * scale * gain).astype(BF16)
-        pltpu.make_async_copy(
-            staged.at[u],
-            out_ref.at[
-                pl.ds(pl.multiple_of(c * CHUNK, CHUNK), CHUNK),
-                pl.ds(pl.multiple_of(g * SPAN, SPAN), SPAN),
-            ],
-            out_sem,
-        ).start()
-        return 0
-
-    lax.fori_loop(0, units, finish, 0)
+        lax.fori_loop(0, CHUNKS, finish, 0)
 
     def drain(c, _):
         peers = recv.at[c, pl.ds(0, n - 1)]
@@ -430,8 +455,8 @@
 
     lax.fori_loop(0, CHUNKS, drain, 0)
     pltpu.make_async_copy(extras, extras, extra_send).wait()
-    wait_all(own, scan_send, MESSAGE)
-    wait_all(prefix, back_send, HEAD_DIM)
+    wait_messages(own, n - 1, MESSAGE, scan_send)
+    wait_messages(prefix, n - 1, HEAD_DIM, back_send)
     pltpu.make_async_copy(staged, staged, out_sem).wait()
 
 
@@ -487,9 +512,10 @@
             pltpu.VMEM((heads * MESSAGE, STATE_WIDTH), BF16),
             pltpu.VMEM((heads * HEAD_DIM, STATE_WIDTH), BF16),
             pltpu.VMEM((heads * HEAD_DIM, STATE_WIDTH), BF16),
+            pltpu.VMEM((STATE_WIDTH, SPAN), BF16),
             pltpu.VMEM((units, CHUNK, SPAN), BF16),
             dma((CHUNKS,)), dma((CHUNKS,)), dma((CHUNKS,)), dma, dma, dma, dma,
-            dma, dma, dma, dma, dma, dma,
+            dma, dma, dma, dma((GROUPS,)), dma, dma,
         ],
         compiler_params=pltpu.CompilerParams(
             collective_id=0, has_side_effects=True, vmem_limit_bytes=48 * 2**20

time: 147 us -> 143 us (0.973)
  Pallas kernels: 143 us -> 139 us
    pallas_call x1, Pallas kernels: 143 us -> 139 us  [per_device(): pl.pallas_call(functools.partial(kernel, n), out_shape=jax.ShapeDtypeStru...]
where the time goes in v4:
time: 143 us
  Pallas kernels  139 us (97%)
  local copies, waits for them, and re-layouts  2.83 us (2%)
    pallas_call x1, Pallas kernels, per_device(): pl.pallas_call(functools.partial(kernel, n), out_shape=jax.ShapeDtypeStru...  139 us

profile of v4, /device:TPU:1, one launch (start us, length us, event | category | flops | bytes accessed | tf_op | source)
XLA Modules:
  0.0 142.8 jit_solution(8687916902198358894)
XLA Ops:
  0.0 0.7 select_maximum_fusion
  0.7 0.8 reshape.6
  1.5 0.7 pad_maximum_fusion.pack_hbm
  2.2 138.6 %shard_map.64 = bf16[1024,2048]{1,0:T(8,128)(2,1)S(1)} custom-call(bf16[145,32768]{1,0:T(8,128)(2,1)} %x_ref.1, f32[104,128]{1,0:T(8,128)S(1)} %pad_maximum_fusion.pack_hbm), custom_call_target="tpu_custom_call" | custom-call | tf_op jit(solution)/shard_map/pallas_call | solution.py:481
  140.8 2.0 %copy.8 = bf16[1024,2048]{1,0:T(8,128)(2,1)} copy(bf16[1024,2048]{1,0:T(8,128)(2,1)S(1)} %shard_map.64) | data formatting | bytes 8388608

commit v5 on v4

--- a/solution.py
+++ b/solution.py
@@ -19,7 +19,6 @@
 COLS = SPAN + CONV + HEADS
 EPSILON = 1e-05
 AHEAD = 3
-CONV_ROWS = 4 * GROUPS * CONV // CHUNK
 HELD = 2
 MESSAGE = HEAD_DIM + 16
 
@@ -36,8 +35,8 @@
 
 
 def kernel(
-    n, x_ref, pack_hbm, out_ref,
-    pack_ref, recv, rows, gates, taps, params, prev, act, wgt, state, carried, within, into,
+    n, x_ref, conv_hbm, pack_hbm, out_ref,
+    conv_ref, pack_ref, recv, rows, gates, taps, params, prev, act, wgt, state, carried, within, into,
     outmap, outrows, small, lead, turned_gate, turned_own,
     tails, spare, extra_out, extra_in, extra, own, gathered, prefix, incoming, turned_in, staged,
     chunk_send, chunk_recv, chunk_own, extra_send, extra_recv, tail_sem, spare_sem,
@@ -48,8 +47,12 @@
     body = slab - 1
     per_group = n // GROUPS
 
-    load = pltpu.make_async_copy(pack_hbm, pack_ref, small_sem)
-    load.start()
+    loads = (
+        pltpu.make_async_copy(pack_hbm, pack_ref, small_sem.at[0]),
+        pltpu.make_async_copy(conv_hbm, conv_ref, small_sem.at[1]),
+    )
+    for load in loads:
+        load.start()
     spare_load = pltpu.make_async_copy(x_ref.at[pl.ds(body, 1), :], spare, spare_sem)
     spare_load.start()
 
@@ -74,7 +77,7 @@
     pl.semaphore_wait(barrier, n - 1)
 
     def peer(i, shift):
-        move = lax.rem(i * 11 + shift, n - 1) + 1
+        move = lax.rem(i * 17 + shift, n - 1) + 1
         if n != 32:
             return lax.rem(me + move, n)
         y = lax.rem(me // 8 + move // 8, 4)
@@ -89,7 +92,7 @@
     def send_chunk(c, _):
 
         def send(i, _):
-            device = peer(i, c * 5)
+            device = peer(i, c * 2)
             pltpu.make_async_remote_copy(
                 src_ref=piece(device, c),
                 dst_ref=recv.at[c, me],
@@ -155,12 +158,13 @@
     lane = lax.broadcasted_iota(jnp.int32, (CHUNK, CHUNK), 1)
     causal = sub <= lane
 
-    load.wait()
+    for load in loads:
+        load.wait()
 
     def taps_of(g, i):
         four = jnp.concatenate(
             [
-                pack_ref[pl.ds((k * GROUPS + g) * (CONV // CHUNK) + i, 1), :]
+                conv_ref[k, g : g + 1, i * CHUNK : (i + 1) * CHUNK]
                 for k in range(4)
             ]
             + [jnp.zeros((CHUNK - 4, CHUNK), F32)],
@@ -176,7 +180,10 @@
         for i in range(CONV // CHUNK):
             taps_of(g, i)
     rows[0:CHUNK, :] = jnp.zeros((CHUNK, CHUNK), F32)
-    rows[0:8, :] = pack_ref[CONV_ROWS : CONV_ROWS + 8, :]
+    for k in range(3):
+        rows[k : k + 1, 0 : GROUPS * HEADS] = pack_ref[
+            0:1, k * GROUPS * HEADS : (k + 1) * GROUPS * HEADS
+        ]
     turned = jnp.transpose(rows[0:CHUNK, :])
     for k in range(3):
         for g in range(GROUPS):
@@ -422,7 +429,7 @@
             turned_in[:, i * CHUNK : (i + 1) * CHUNK] = jnp.transpose(block.astype(F32)).astype(
                 BF16
             )
-        first = CONV_ROWS + 8 + g * (SPAN // CHUNK)
+        first = 1 + g * (SPAN // CHUNK)
         gain = jnp.concatenate(
             [pack_ref[first + i : first + i + 1, :] for i in range(SPAN // CHUNK)], axis=1
         )
@@ -466,24 +473,19 @@
     tokens = CHUNK * CHUNKS
     units = GROUPS * CHUNKS
     heads = GROUPS * HEADS
-    scalars = jnp.stack([dt_bias, a_log, d_skip])
     packed = jnp.concatenate(
-        [
-            conv_weight.reshape(-1, CHUNK),
-            jnp.pad(scalars, ((0, 5), (0, CHUNK - heads))),
-            norm_gain.reshape(-1, CHUNK),
-        ],
-        axis=0,
-    )
+        [dt_bias, a_log, d_skip, jnp.zeros((heads,), F32), norm_gain]
+    ).reshape(-1, CHUNK)
     hbm = pl.BlockSpec(memory_space=pltpu.HBM)
     anywhere = pl.BlockSpec(memory_space=pl.ANY)
     dma = pltpu.SemaphoreType.DMA
     return pl.pallas_call(
         functools.partial(kernel, n),
         out_shape=jax.ShapeDtypeStruct((tokens, GROUPS * SPAN), BF16),
-        in_specs=[hbm] * 2,
+        in_specs=[hbm] * 3,
         out_specs=anywhere,
         scratch_shapes=[
+            pltpu.VMEM((4, GROUPS, CONV), F32),
             pltpu.VMEM(packed.shape, F32),
             pltpu.VMEM((CHUNKS, n, slab - 1, CHUNK), BF16),
             pltpu.VMEM((COLS, CHUNK), F32),
@@ -515,13 +517,13 @@
             pltpu.VMEM((STATE_WIDTH, SPAN), BF16),
             pltpu.VMEM((units, CHUNK, SPAN), BF16),
             dma((CHUNKS,)), dma((CHUNKS,)), dma((CHUNKS,)), dma, dma, dma, dma,
-            dma, dma, dma, dma((GROUPS,)), dma, dma,
+            dma, dma, dma, dma((GROUPS,)), dma, dma((2,)),
         ],
         compiler_params=pltpu.CompilerParams(
             collective_id=0, has_side_effects=True, vmem_limit_bytes=48 * 2**20
         ),
     )(
-        projected, packed
+        projected, conv_weight, packed
     )
 
 

time: 143 us -> 140 us (0.979)
  Pallas kernels: 139 us -> 136 us
    pallas_call x1, Pallas kernels: 139 us -> 136 us  [per_device(): pl.pallas_call(functools.partial(kernel, n), out_shape=jax.ShapeDtypeStru...]
where the time goes in v5:
time: 140 us
  Pallas kernels  136 us (97%)
  local copies, waits for them, and re-layouts  3.62 us (3%)
    pallas_call x1, Pallas kernels, per_device(): pl.pallas_call(functools.partial(kernel, n), out_shape=jax.ShapeDtypeStru...  136 us

profile of v5, /device:TPU:1, one launch (start us, length us, event | category | flops | bytes accessed | tf_op | source)
XLA Modules:
  0.0 139.9 jit_solution(7971878298402335026)
XLA Ops:
  0.0 0.8 concatenate.3
  0.8 0.0 copy-start
  0.8 0.8 copy-done
  1.6 136.3 %shard_map.64 = bf16[1024,2048]{1,0:T(8,128)(2,1)S(1)} custom-call(bf16[145,32768]{1,0:T(8,128)(2,1)} %x_ref.1, f32[4,2,1280]{2,1,0:T(2,128)S(1)} %copy-done, f32[17,128]{1,0:T(8,128)S(1)} %bitcast.1), custom_call_target="tpu_custom_call" | custom-call | tf_op jit(solution)/shard_map/pallas_call | solution.py:482
  137.9 2.0 %copy.8 = bf16[1024,2048]{1,0:T(8,128)(2,1)} copy(bf16[1024,2048]{1,0:T(8,128)(2,1)S(1)} %shard_map.64) | data formatting | bytes 8388608
  (1 shorter events, 0.0 us)
Async XLA Ops:
  0.8 0.8 copy-start

commit v6 on v5

--- a/solution.py
+++ b/solution.py
@@ -377,7 +377,7 @@
 
             return 0
 
-        lax.fori_loop(0, HEADS, send_state, 0)
+        lax.fori_loop(0, HEADS, send_state, 0, unroll=True)
     head_at(gathered, me, MESSAGE)[...] = head_at(own, me, MESSAGE)[...]
 
     @pl.when(mine == 1)
@@ -392,7 +392,7 @@
         fade = jnp.sum(message[HEAD_DIM:, :], axis=0, keepdims=True)
         return reached * fade + message[:HEAD_DIM, :]
 
-    lax.fori_loop(0, n, horner, jnp.zeros((HEAD_DIM, STATE_WIDTH), F32))
+    lax.fori_loop(0, n, horner, jnp.zeros((HEAD_DIM, STATE_WIDTH), F32), unroll=8)
     slot = mine * HEADS + me // GROUPS
 
     def send_back(i, _):
@@ -407,7 +407,7 @@
         ).start()
         return 0
 
-    lax.fori_loop(0, n - 1, send_back, 0)
+    lax.fori_loop(0, n - 1, send_back, 0, unroll=True)
     head_at(incoming, slot, HEAD_DIM)[...] = head_at(prefix, me, HEAD_DIM)[...]
 
     @pl.when(mine == 0)

time: 140 us -> 140 us (level)
  no operation moved by 1% of the time
where the time goes in v6:
time: 140 us; the launch traced here: 139 us
  Pallas kernels  136 us (97%)
  local copies, waits for them, and re-layouts  3.62 us (3%)
    pallas_call x1, Pallas kernels, per_device(): pl.pallas_call(functools.partial(kernel, n), out_shape=jax.ShapeDtypeStru...  136 us

profile of v6, /device:TPU:1, one launch (start us, length us, event | category | flops | bytes accessed | tf_op | source)
XLA Modules:
  0.0 139.2 jit_solution(4266035826721504024)
XLA Ops:
  0.0 0.8 concatenate.3
  0.8 0.0 copy-start
  0.8 0.8 copy-done
  1.6 135.6 %shard_map.64 = bf16[1024,2048]{1,0:T(8,128)(2,1)S(1)} custom-call(bf16[145,32768]{1,0:T(8,128)(2,1)} %x_ref.1, f32[4,2,1280]{2,1,0:T(2,128)S(1)} %copy-done, f32[17,128]{1,0:T(8,128)S(1)} %bitcast.1), custom_call_target="tpu_custom_call" | custom-call | tf_op jit(solution)/shard_map/pallas_call | solution.py:482
  137.2 2.0 %copy.8 = bf16[1024,2048]{1,0:T(8,128)(2,1)} copy(bf16[1024,2048]{1,0:T(8,128)(2,1)S(1)} %shard_map.64) | data formatting | bytes 8388608
  (1 shorter events, 0.0 us)
Async XLA Ops:
  0.8 0.8 copy-start
